TPU v7x, 32 devices: a whole 2x2x4 slice. The times are simulated.
32 devices in a mesh: ctx: 8 (over z, y), fsdp: 4 (over x, core).
Axes of the slice: x: 2, y: 2, z: 4, core: 2. Of those that a mesh axis runs over, the one named last changes fastest.
Arguments:
- tokens: bfloat16 [4, 1280, 1024], P('fsdp', 'ctx')
- lengths: int32 [4, 4], P('fsdp'), may hold values from 1 to 1024, 1280 in all within a row
- deal: int32 [4, 8, 8], P('fsdp'), may hold values from 0 to 7, each once within a row
- attn_gain: bfloat16 [1024], P('fsdp'), may hold values from 0.25 to 1.75
- w_q: bfloat16 [1024, 2048], P('fsdp'), may hold values from -0.1875 to 0.1875
- key_weight: bfloat16 [1024, 1024], P('fsdp'), may hold values from -0.1875 to 0.1875
- value_weight: bfloat16 [1024, 1024], P('fsdp'), may hold values from -0.1875 to 0.1875
- query_norm_gain: bfloat16 [128], P('fsdp'), may hold values from 0.25 to 1.75
- k_gain: bfloat16 [128], P('fsdp'), may hold values from 0.25 to 1.75
- w_o: bfloat16 [2048, 1024], P('fsdp'), may hold values from -0.5 to 0.5
- mlp_gain: bfloat16 [1024], P('fsdp'), may hold values from 0.25 to 1.75
- w_gate: bfloat16 [1024, 3072], P('fsdp'), may hold values from -0.1875 to 0.1875
- w_up: bfloat16 [1024, 3072], P('fsdp'), may hold values from -0.1875 to 0.1875
- w_down: bfloat16 [3072, 1024], P('fsdp'), may hold values from -0.109375 to 0.109375
- out_cotangent: bfloat16 [4, 1280, 1024], P('fsdp', 'ctx'), may hold values from -6 to 6
Outputs:
- output: bfloat16 [4, 1280, 1024], P('fsdp', 'ctx')
- input_grad: float32 [4, 1280, 1024], P('fsdp', 'ctx')
- attn_gain_grad: float32 [1024], P('fsdp')
- q_gain_grad: float32 [128], P('fsdp')
- k_gain_grad: float32 [128], P('fsdp')
- mlp_gain_grad: float32 [1024], P('fsdp')
- w_q_grad: float32 [1024, 2048], P('fsdp')
- w_k_grad: float32 [1024, 1024], P('fsdp')
- w_v_grad: float32 [1024, 1024], P('fsdp')
- w_o_grad: float32 [2048, 1024], P('fsdp')
- w_gate_grad: float32 [1024, 3072], P('fsdp')
- w_up_grad: float32 [1024, 3072], P('fsdp')
- w_down_grad: float32 [3072, 1024], P('fsdp')
Inputs may be any that keep to these rules, and one draw needn't show every extreme that they name: Each group's 4 lengths sum to 1280; the longest is exactly 1024. Each row deal[g, s] names every device of a group once.
All inputs are finite; a program needn't handle non-finite values.
Results may differ from a plain program's by a relative error of at most 0.034.
Values may be sent and summed in bfloat16 or wider, within the bound.
A program may use at most 320 MiB of HBM per device.

v0:
```python
import math

import jax
import jax.numpy as jnp
from jax import lax
from jax.sharding import PartitionSpec as P

MODEL_WIDTH = 1024
QUERY_HEADS = 16
KEY_VALUE_HEADS = 8
HEAD_SIZE = 128


eps = 1e-06
theta_base = 1000000.0
negative_filler = -1e30


def root_mean_norm(values, gain_vec):
    return values * lax.rsqrt(jnp.mean(values * values, axis=-1, keepdims=True) + eps) * gain_vec


def rotary_embedding(values, token_position):
    half_width = values.shape[-1] // 2
    frequency = theta_base ** (
        -(jnp.arange(half_width, dtype=jnp.float32) * 2.0) / values.shape[-1]
    )
    angles = token_position.astype(jnp.float32)[:, None] * frequency[None, :]
    cosine = jnp.concatenate([jnp.cos(angles), jnp.cos(angles)], axis=-1)[:, None, :]
    sine_part = jnp.concatenate([jnp.sin(angles), jnp.sin(angles)], axis=-1)[:, None, :]
    turned = jnp.concatenate([-values[..., half_width:], values[..., :half_width]], axis=-1)
    return values * cosine + turned * sine_part


def dot_trans(left_side, right_side):
    return lax.dot_general(
        left_side, right_side, (((1,), (1,)), ((), ())), preferred_element_type=jnp.float32
    )


def outer_rows(left_side, right_side):
    return lax.dot_general(
        left_side, right_side, (((0,), (0,)), ((), ())), preferred_element_type=jnp.float32
    )


def block_plan(piece_rows, local_rows):
    shards = piece_rows // local_rows
    per_block = math.gcd(shards, max(1, 1024 // local_rows))
    return (per_block * local_rows, shards // per_block)


def over_blocks(carried, arrays, local_rows, block_work):
    rows_per_block, count_of_blocks = block_plan(arrays[0].shape[0], local_rows)

    def one_block(turn_index, state_now):
        offset = turn_index * rows_per_block
        parts = tuple(
            (lax.dynamic_slice_in_dim(member, offset, rows_per_block, 0) for member in arrays)
        )
        return block_work(state_now, parts, offset)

    return lax.fori_loop(0, count_of_blocks, one_block, carried)


def segment_begin(tok_ids, starts):
    return jnp.max(jnp.where(tok_ids[:, None] >= starts[None, :], starts[None, :], 0), axis=1)


def on_device(
    tokens,
    lengths,
    deal,
    attn_gain,
    w_q,
    key_weight,
    value_weight,
    query_norm_gain,
    k_gain,
    w_o,
    mlp_gain,
    w_gate,
    w_up,
    w_down,
    out_cotangent,
):
    local_rows = tokens.shape[1]
    piece_count = lax.axis_size("ctx")
    piece_rows = local_rows // piece_count
    here = lax.axis_index("ctx")
    group_width = QUERY_HEADS // KEY_VALUE_HEADS
    score_scale = HEAD_SIZE ** (-0.5)
    seq_lengths = lengths[0]
    starts = jnp.cumsum(seq_lengths) - seq_lengths
    plan = deal[0]
    devices = jnp.arange(piece_count, dtype=jnp.int32)
    hits = plan[:, :, None] == devices[None, None, :]
    slot_of = jnp.sum(jnp.where(hits, devices[None, :, None], 0), axis=1)
    inner = jnp.arange(piece_rows, dtype=jnp.int32)
    dealt_index = (
        devices[None, :, None] * local_rows
        + jnp.transpose(slot_of)[:, :, None] * piece_rows
        + inner[None, None, :]
    ).reshape(piece_count * local_rows)
    dealt_first = segment_begin(dealt_index, starts)
    tok_index = lax.dynamic_slice_in_dim(dealt_index, here * local_rows, local_rows)
    segment_initial = lax.dynamic_slice_in_dim(dealt_first, here * local_rows, local_rows)
    token_position = tok_index - segment_initial
    own_slots = lax.dynamic_index_in_dim(slot_of, here, 0, keepdims=False)
    own_plan = lax.dynamic_index_in_dim(plan, here, 0, keepdims=False)
    token_pieces = jnp.take(
        tokens[0].reshape(piece_count, piece_rows, MODEL_WIDTH), own_slots, axis=0
    )
    dealt_tok = lax.all_to_all(
        token_pieces, "ctx", split_axis=0, concat_axis=0, tiled=True
    ).reshape(local_rows, MODEL_WIDTH)

    def key_mask(start_row, local_row_count):
        key_identifiers = lax.dynamic_slice_in_dim(dealt_index, start_row, local_row_count)
        return (key_identifiers[None, :] >= segment_initial[:, None]) & (
            key_identifiers[None, :] <= tok_index[:, None]
        )

    def query_mask(start_row, local_row_count):
        query_ids = lax.dynamic_slice_in_dim(dealt_index, start_row, local_row_count)
        first_key = lax.dynamic_slice_in_dim(dealt_first, start_row, local_row_count)
        return (tok_index[None, :] >= first_key[:, None]) & (
            tok_index[None, :] <= query_ids[:, None]
        )

    def fetch_weights():
        attn_set = (
            lax.all_gather(attn_gain, "fsdp", axis=0, tiled=True),
            lax.all_gather(query_norm_gain, "fsdp", axis=0, tiled=True),
            lax.all_gather(k_gain, "fsdp", axis=0, tiled=True),
            lax.all_gather(w_q, "fsdp", axis=0, tiled=True),
            lax.all_gather(key_weight, "fsdp", axis=0, tiled=True),
            lax.all_gather(value_weight, "fsdp", axis=0, tiled=True),
            lax.all_gather(w_o, "fsdp", axis=0, tiled=True),
        )
        mlp_set = (
            lax.all_gather(mlp_gain, "fsdp", axis=0, tiled=True),
            lax.all_gather(w_gate, "fsdp", axis=0, tiled=True),
            lax.all_gather(w_up, "fsdp", axis=0, tiled=True),
            lax.all_gather(w_down, "fsdp", axis=0, tiled=True),
        )
        return (attn_set, mlp_set)

    def forward(attn_set, mlp_set, token_rows):
        a_gain, qn_gain, kn_gain, proj_q, proj_k, proj_v, proj_o = attn_set
        m_gain, proj_gate, proj_up, proj_down = mlp_set
        residual = token_rows.astype(jnp.float32)
        normalized_input = root_mean_norm(residual, a_gain.astype(jnp.float32)).astype(jnp.bfloat16)
        query_prenorm = jnp.dot(
            normalized_input, proj_q, preferred_element_type=jnp.float32
        ).reshape(local_rows, QUERY_HEADS, HEAD_SIZE)
        key_prenorm = jnp.dot(normalized_input, proj_k, preferred_element_type=jnp.float32).reshape(
            local_rows, KEY_VALUE_HEADS, HEAD_SIZE
        )
        value_narrow = jnp.dot(normalized_input, proj_v, preferred_element_type=jnp.float32).astype(
            jnp.bfloat16
        )
        q_heads = (
            rotary_embedding(
                root_mean_norm(query_prenorm, qn_gain.astype(jnp.float32)), token_position
            )
            .astype(jnp.bfloat16)
            .reshape(local_rows, KEY_VALUE_HEADS, group_width, HEAD_SIZE)
        )
        key_narrow = (
            rotary_embedding(
                root_mean_norm(key_prenorm, kn_gain.astype(jnp.float32)), token_position
            )
            .astype(jnp.bfloat16)
            .reshape(local_rows, KEY_VALUE_HEADS * HEAD_SIZE)
        )

        def attend_over_block(state_now, shard_piece, start_row):
            key_segment, value_segment = shard_piece
            local_row_count = key_segment.shape[0]
            allowed = key_mask(start_row, local_row_count)
            row_top, row_total, weighted = state_now
            scores = (
                jnp.einsum(
                    "rkgh,ckh->kgrc",
                    q_heads,
                    key_segment.reshape(local_row_count, KEY_VALUE_HEADS, HEAD_SIZE),
                    preferred_element_type=jnp.float32,
                )
                * score_scale
            )
            scores = jnp.where(allowed, scores, negative_filler)
            new_top = jnp.maximum(row_top, jnp.max(scores, axis=-1))
            rescale = jnp.exp(row_top - new_top)
            weights = jnp.where(allowed, jnp.exp(scores - new_top[..., None]), 0.0)
            row_total = row_total * rescale + jnp.sum(weights, axis=-1)
            weighted = weighted * rescale[..., None] + jnp.einsum(
                "kgrc,ckh->kgrh",
                weights.astype(jnp.bfloat16),
                value_segment.reshape(local_row_count, KEY_VALUE_HEADS, HEAD_SIZE),
                preferred_element_type=jnp.float32,
            )
            return (new_top, row_total, weighted)

        initial = (
            jnp.full((KEY_VALUE_HEADS, group_width, local_rows), negative_filler, jnp.float32),
            jnp.zeros((KEY_VALUE_HEADS, group_width, local_rows), jnp.float32),
            jnp.zeros((KEY_VALUE_HEADS, group_width, local_rows, HEAD_SIZE), jnp.float32),
        )
        row_top, row_total, weighted = over_blocks(
            initial,
            (
                lax.all_gather(key_narrow, "ctx", axis=0, tiled=True),
                lax.all_gather(value_narrow, "ctx", axis=0, tiled=True),
            ),
            local_rows,
            attend_over_block,
        )
        attention_mixed = jnp.transpose(weighted / row_total[..., None], (2, 0, 1, 3)).reshape(
            local_rows, QUERY_HEADS * HEAD_SIZE
        )
        log_total = row_top + jnp.log(row_total)
        mixed_low = attention_mixed.astype(jnp.bfloat16)
        middle = residual + jnp.dot(mixed_low, proj_o, preferred_element_type=jnp.float32)
        normed2 = root_mean_norm(middle, m_gain.astype(jnp.float32)).astype(jnp.bfloat16)
        gate_pre = jnp.dot(normed2, proj_gate, preferred_element_type=jnp.float32)
        up_pre = jnp.dot(normed2, proj_up, preferred_element_type=jnp.float32)
        hidden = (jax.nn.silu(gate_pre) * up_pre).astype(jnp.bfloat16)
        result = middle + jnp.dot(hidden, proj_down, preferred_element_type=jnp.float32)
        return (
            result,
            residual,
            normalized_input,
            query_prenorm,
            key_prenorm,
            value_narrow,
            q_heads,
            key_narrow,
            attention_mixed,
            mixed_low,
            log_total,
            middle,
            normed2,
            gate_pre,
            up_pre,
            hidden,
            attn_set,
            mlp_set,
        )

    first_sets = fetch_weights()
    first_pass = forward(first_sets[0], first_sets[1], dealt_tok)
    again_tok = lax.all_to_all(
        token_pieces, "ctx", split_axis=0, concat_axis=0, tiled=True
    ).reshape(local_rows, MODEL_WIDTH)
    second_sets = fetch_weights()
    kept_pass = forward(second_sets[0], second_sets[1], again_tok)
    (
        unused,
        residual,
        normalized_input,
        query_prenorm,
        key_prenorm,
        value_narrow,
        q_heads,
        key_narrow,
        attention_mixed,
        mixed_low,
        log_total,
        middle,
        normed2,
        gate_pre,
        up_pre,
        hidden,
        attn_set,
        mlp_set,
    ) = kept_pass
    a_gain, qn_gain, kn_gain, proj_q, proj_k, proj_v, proj_o = attn_set
    m_gain, proj_gate, proj_up, proj_down = mlp_set
    grad_low = out_cotangent[0]
    grad_out = grad_low.astype(jnp.float32)
    d_hidden = dot_trans(grad_low, proj_down)
    down_grad = lax.psum_scatter(
        outer_rows(hidden, grad_low).astype(jnp.bfloat16), "fsdp", scatter_dimension=0, tiled=True
    )
    unused, swiglu_back = jax.vjp(
        lambda gate_in, up_in: jax.nn.silu(gate_in) * up_in, gate_pre, up_pre
    )
    d_gate, d_up = swiglu_back(d_hidden)
    d_gate_low = d_gate.astype(jnp.bfloat16)
    d_up_low = d_up.astype(jnp.bfloat16)
    d_normed2 = dot_trans(d_gate_low, proj_gate) + dot_trans(d_up_low, proj_up)
    both_low = jnp.concatenate([d_gate_low, d_up_low], axis=1)
    gate_up_grad = lax.psum_scatter(
        outer_rows(normed2, both_low).astype(jnp.bfloat16), "fsdp", scatter_dimension=0, tiled=True
    )
    unused, norm2_back = jax.vjp(root_mean_norm, middle, m_gain.astype(jnp.float32))
    d_middle_norm, d_m_gain = norm2_back(d_normed2)
    d_middle = grad_out + d_middle_norm
    middle_low = d_middle.astype(jnp.bfloat16)
    mixed_gradient = dot_trans(middle_low, proj_o).astype(jnp.bfloat16)
    out_proj_grad = lax.psum_scatter(
        outer_rows(mixed_low, middle_low).astype(jnp.bfloat16),
        "fsdp",
        scatter_dimension=0,
        tiled=True,
    )
    heads_gradient = mixed_gradient.reshape(local_rows, KEY_VALUE_HEADS, group_width, HEAD_SIZE)
    delta_rows = jnp.sum(
        heads_gradient.astype(jnp.float32)
        * attention_mixed.reshape(local_rows, KEY_VALUE_HEADS, group_width, HEAD_SIZE),
        axis=-1,
    )
    delta_t = jnp.transpose(delta_rows, (1, 2, 0))
    local_keys = key_narrow.reshape(local_rows, KEY_VALUE_HEADS, HEAD_SIZE)
    local_values = value_narrow.reshape(local_rows, KEY_VALUE_HEADS, HEAD_SIZE)

    def query_block(state_now, shard_piece, start_row):
        key_segment, value_segment = shard_piece
        local_row_count = key_segment.shape[0]
        allowed = key_mask(start_row, local_row_count)
        key_row_block = key_segment.reshape(local_row_count, KEY_VALUE_HEADS, HEAD_SIZE)
        scores = (
            jnp.einsum("rkgh,ckh->kgrc", q_heads, key_row_block, preferred_element_type=jnp.float32)
            * score_scale
        )
        probability = jnp.where(allowed, jnp.exp(scores - log_total[..., None]), 0.0)
        d_probs = jnp.einsum(
            "rkgh,ckh->kgrc",
            heads_gradient,
            value_segment.reshape(local_row_count, KEY_VALUE_HEADS, HEAD_SIZE),
            preferred_element_type=jnp.float32,
        )
        d_scores = (probability * (d_probs - delta_t[..., None])).astype(jnp.bfloat16)
        return (
            state_now
            + jnp.einsum(
                "kgrc,ckh->kgrh", d_scores, key_row_block, preferred_element_type=jnp.float32
            )
            * score_scale
        )

    query_grad = over_blocks(
        jnp.zeros((KEY_VALUE_HEADS, group_width, local_rows, HEAD_SIZE), jnp.float32),
        (
            lax.all_gather(key_narrow, "ctx", axis=0, tiled=True),
            lax.all_gather(value_narrow, "ctx", axis=0, tiled=True),
        ),
        local_rows,
        query_block,
    )
    lse_rows = jnp.transpose(log_total, (2, 0, 1)).reshape(local_rows, QUERY_HEADS)
    delta_send = delta_rows.reshape(local_rows, QUERY_HEADS)

    def key_block(state_now, shard_piece, start_row):
        query_segment, output_gradient_segment, logsumexp_segment, delta_segment = shard_piece
        local_row_count = query_segment.shape[0]
        allowed = query_mask(start_row, local_row_count)
        key_grad, value_gradient = state_now
        query_matrix = query_segment.reshape(
            local_row_count, KEY_VALUE_HEADS, group_width, HEAD_SIZE
        )
        gradient_rows = output_gradient_segment.reshape(
            local_row_count, KEY_VALUE_HEADS, group_width, HEAD_SIZE
        )
        scores = (
            jnp.einsum(
                "ckgh,rkh->kgcr", query_matrix, local_keys, preferred_element_type=jnp.float32
            )
            * score_scale
        )
        logsumexp_portion = jnp.transpose(
            logsumexp_segment.reshape(local_row_count, KEY_VALUE_HEADS, group_width), (1, 2, 0)
        )
        delta_portion = jnp.transpose(
            delta_segment.reshape(local_row_count, KEY_VALUE_HEADS, group_width), (1, 2, 0)
        )
        probability = jnp.where(allowed, jnp.exp(scores - logsumexp_portion[..., None]), 0.0)
        value_gradient = value_gradient + jnp.einsum(
            "kgcr,ckgh->rkh",
            probability.astype(jnp.bfloat16),
            gradient_rows,
            preferred_element_type=jnp.float32,
        )
        d_probs = jnp.einsum(
            "ckgh,rkh->kgcr", gradient_rows, local_values, preferred_element_type=jnp.float32
        )
        d_scores = (probability * (d_probs - delta_portion[..., None])).astype(jnp.bfloat16)
        key_grad = (
            key_grad
            + jnp.einsum(
                "kgcr,ckgh->rkh", d_scores, query_matrix, preferred_element_type=jnp.float32
            )
            * score_scale
        )
        return (key_grad, value_gradient)

    key_grad, value_gradient = over_blocks(
        (
            jnp.zeros((local_rows, KEY_VALUE_HEADS, HEAD_SIZE), jnp.float32),
            jnp.zeros((local_rows, KEY_VALUE_HEADS, HEAD_SIZE), jnp.float32),
        ),
        (
            lax.all_gather(
                q_heads.reshape(local_rows, QUERY_HEADS * HEAD_SIZE), "ctx", axis=0, tiled=True
            ),
            lax.all_gather(mixed_gradient, "ctx", axis=0, tiled=True),
            lax.all_gather(lse_rows.astype(jnp.bfloat16), "ctx", axis=0, tiled=True).astype(
                jnp.float32
            ),
            lax.all_gather(delta_send.astype(jnp.bfloat16), "ctx", axis=0, tiled=True).astype(
                jnp.float32
            ),
        ),
        local_rows,
        key_block,
    )
    query_rows = jnp.transpose(query_grad, (2, 0, 1, 3)).reshape(local_rows, QUERY_HEADS, HEAD_SIZE)
    unused, q_back = jax.vjp(
        lambda head_in, gain_in: rotary_embedding(root_mean_norm(head_in, gain_in), token_position),
        query_prenorm,
        qn_gain.astype(jnp.float32),
    )
    d_q_pre, d_qn_gain = q_back(query_rows)
    unused, k_back = jax.vjp(
        lambda head_in, gain_in: rotary_embedding(root_mean_norm(head_in, gain_in), token_position),
        key_prenorm,
        kn_gain.astype(jnp.float32),
    )
    key_prenorm_gradient, d_kn_gain = k_back(key_grad)
    dq_low = d_q_pre.reshape(local_rows, QUERY_HEADS * HEAD_SIZE).astype(jnp.bfloat16)
    key_gradient_narrow = key_prenorm_gradient.reshape(
        local_rows, KEY_VALUE_HEADS * HEAD_SIZE
    ).astype(jnp.bfloat16)
    value_gradient_narrow = value_gradient.reshape(local_rows, KEY_VALUE_HEADS * HEAD_SIZE).astype(
        jnp.bfloat16
    )
    d_normed = (
        dot_trans(dq_low, proj_q)
        + dot_trans(key_gradient_narrow, proj_k)
        + dot_trans(value_gradient_narrow, proj_v)
    )
    qkv_low = jnp.concatenate([dq_low, key_gradient_narrow, value_gradient_narrow], axis=1)
    qkv_grad = lax.psum_scatter(
        outer_rows(normalized_input, qkv_low).astype(jnp.bfloat16),
        "fsdp",
        scatter_dimension=0,
        tiled=True,
    )
    unused, norm1_back = jax.vjp(root_mean_norm, residual, a_gain.astype(jnp.float32))
    d_resid_norm, d_a_gain = norm1_back(d_normed)
    input_dealt = d_middle + d_resid_norm
    back_pieces = lax.all_to_all(
        input_dealt.reshape(piece_count, piece_rows, MODEL_WIDTH).astype(jnp.bfloat16),
        "ctx",
        split_axis=0,
        concat_axis=0,
        tiled=True,
    ).astype(jnp.float32)
    input_grad = jnp.take(back_pieces, own_plan, axis=0).reshape(local_rows, MODEL_WIDTH)
    gain_parts = (
        lax.psum_scatter(d_a_gain, "fsdp", scatter_dimension=0, tiled=True),
        lax.psum_scatter(d_qn_gain, "fsdp", scatter_dimension=0, tiled=True),
        lax.psum_scatter(d_kn_gain, "fsdp", scatter_dimension=0, tiled=True),
        lax.psum_scatter(d_m_gain, "fsdp", scatter_dimension=0, tiled=True),
    )
    totals = (
        lax.psum(gain_parts[0].astype(jnp.bfloat16), "ctx").astype(jnp.float32),
        lax.psum(gain_parts[1].astype(jnp.bfloat16), "ctx").astype(jnp.float32),
        lax.psum(gain_parts[2].astype(jnp.bfloat16), "ctx").astype(jnp.float32),
        lax.psum(gain_parts[3].astype(jnp.bfloat16), "ctx").astype(jnp.float32),
        lax.psum(qkv_grad, "ctx").astype(jnp.float32),
        lax.psum(out_proj_grad, "ctx").astype(jnp.float32),
        lax.psum(gate_up_grad, "ctx").astype(jnp.float32),
        lax.psum(down_grad, "ctx").astype(jnp.float32),
    )
    q_width = QUERY_HEADS * HEAD_SIZE
    key_value_width = KEY_VALUE_HEADS * HEAD_SIZE
    qkv_total = totals[4]
    gate_up_total = totals[6]
    ff_width = w_gate.shape[1]
    return (
        first_pass[0].astype(jnp.bfloat16)[None],
        input_grad[None],
        totals[0],
        totals[1],
        totals[2],
        totals[3],
        qkv_total[:, :q_width],
        qkv_total[:, q_width : q_width + key_value_width],
        qkv_total[:, q_width + key_value_width :],
        totals[5],
        gate_up_total[:, :ff_width],
        gate_up_total[:, ff_width:],
        totals[7],
    )


def solution(mesh):
    return jax.shard_map(
        on_device,
        mesh=mesh,
        in_specs=(
            P("fsdp", "ctx", None),
            P("fsdp", None),
            P("fsdp", None, None),
            P("fsdp"),
            P("fsdp", None),
            P("fsdp", None),
            P("fsdp", None),
            P("fsdp"),
            P("fsdp"),
            P("fsdp", None),
            P("fsdp"),
            P("fsdp", None),
            P("fsdp", None),
            P("fsdp", None),
            P("fsdp", "ctx", None),
        ),
        out_specs=(
            P("fsdp", "ctx", None),
            P("fsdp", "ctx", None),
            P("fsdp"),
            P("fsdp"),
            P("fsdp"),
            P("fsdp"),
            P("fsdp", None),
            P("fsdp", None),
            P("fsdp", None),
            P("fsdp", None),
            P("fsdp", None),
            P("fsdp", None),
            P("fsdp", None),
        ),
        check_vma=False,
    )
```

profile of v0, /device:TPU:0, one launch (start us, length us, event | category | flops | bytes accessed | tf_op | source)
XLA Modules:
  0.0 1135.5 jit_solution(2724079580650645476)
XLA Ops:
  11.7 7.3 all-to-all-start
  28.4 7.1 all-reduce.13
  44.8 14.3 %all-gather.22.cloned.1.call-done = bf16[1024,1024]{1,0:T(8,128)(2,1)} async-done(((bf16[256,1024]{1,0:T(8,128)(2,1)}), bf16[1024,1024]{1,0:T(8,128)(2,1)}) %all-gather.22.cloned.1.call-update) | async-done | bytes 2097168 | tf_op jit(solution)/shard_map/all_gather | solution.py:138
  70.7 24.6 %all-gather.20.cloned.1.call-done = bf16[1024,2048]{1,0:T(8,128)(2,1)} async-done(((bf16[256,2048]{1,0:T(8,128)(2,1)}), bf16[1024,2048]{1,0:T(8,128)(2,1)}) %all-gather.20.cloned.1.call-update) | async-done | bytes 4194320 | tf_op jit(solution)/shard_map/all_gather | solution.py:136
  95.2 6.4 copy.141
  108.7 43.9 %all-gather.18.cloned.1.call-done = bf16[1280,1024]{1,0:T(8,128)(2,1)} async-done(((bf16[160,1024]{1,0:T(8,128)(2,1)}), bf16[1280,1024]{1,0:T(8,128)(2,1)}) %all-gather.18.cloned.1.call-update) | async-done | bytes 2621456 | tf_op jit(solution)/shard_map/all_gather | solution.py:213
  152.6 55.3 %all-gather.24.cloned.1.call-done = bf16[1280,1024]{1,0:T(8,128)(2,1)} async-done(((bf16[160,1024]{1,0:T(8,128)(2,1)}), bf16[1280,1024]{1,0:T(8,128)(2,1)}) %all-gather.24.cloned.1.call-update) | async-done | bytes 2621456 | tf_op jit(solution)/shard_map/all_gather | solution.py:214
  207.8 52.4 %while.55 = (s32[]{:T(128)}, f32[8,2,160]{2,1,0:T(2,128)S(1)}, f32[8,2,160]{2,1,0:T(2,128)S(1)}, f32[8,2,160,128]{3,2,1,0:T(8,128)}, s32[1280]{0:T(1024)}, /*ind...) while((s32[]{:T(128)}, f32[8,2,160]{2,1,0:T(2,128)S(1)}, ...), condition=%wide.region_9.10_spmd.clone, body=%wide.region_6.9_spmd.clone.sunk | while | flops 431229440 | bytes 43627808 | solution.py:63
  268.2 22.2 %all-gather.28.cloned.1.call-done = bf16[1024,3072]{1,0:T(8,128)(2,1)} async-done(((bf16[256,3072]{1,0:T(8,128)(2,1)}), bf16[1024,3072]{1,0:T(8,128)(2,1)}) %all-gather.28.cloned.1.call-update) | async-done | bytes 6291472 | tf_op jit(solution)/shard_map/all_gather | solution.py:143
  295.7 42.6 %all-gather.30.cloned.1.call-done = bf16[1024,3072]{1,0:T(8,128)(2,1)} async-done(((bf16[256,3072]{1,0:T(8,128)(2,1)}), bf16[1024,3072]{1,0:T(8,128)(2,1)}) %all-gather.30.cloned.1.call-update) | async-done | bytes 6291472 | tf_op jit(solution)/shard_map/all_gather | solution.py:144
  343.7 42.6 %all-gather.32.cloned.1.call-done = bf16[3072,1024]{1,0:T(8,128)(2,1)} async-done(((bf16[768,1024]{1,0:T(8,128)(2,1)}), bf16[3072,1024]{1,0:T(8,128)(2,1)}) %all-gather.32.cloned.1.call-update) | async-done | bytes 6291472 | tf_op jit(solution)/shard_map/all_gather | solution.py:145
  386.3 7.7 multiply_convert_fusion
  406.8 9.9 reduce-scatter.7.cloned.1.call-start
  428.9 8.0 convolution_convert_fusion
  439.2 31.0 %all-gather.2 = bf16[8,160,16]{1,2,0:T(8,128)(2,1)S(1)} all-gather(bf16[1,160,16]{1,2,0:T(8,128)(2,1)S(1)} %reshape.429), channel_id=1, replica_groups=mesh['ctx'=8,'fsdp'=4] {'ctx'}, dimensions={0}, use_global_device_ids=true | all-gather | bytes 46080 | tf_op jit(solution)/shard_map/all_gather | solution.py:408
  476.7 30.8 %all-gather.3 = bf16[8,160,16]{1,2,0:T(8,128)(2,1)S(1)} all-gather(bf16[1,160,16]{1,2,0:T(8,128)(2,1)S(1)} %reshape.431), channel_id=1, replica_groups=mesh['ctx'=8,'fsdp'=4] {'ctx'}, dimensions={0}, use_global_device_ids=true | all-gather | bytes 46080 | tf_op jit(solution)/shard_map/all_gather | solution.py:411
  508.3 50.2 %while.56 = (s32[]{:T(128)}, f32[8,2,160,128]{3,2,1,0:T(8,128)}, s32[1280]{0:T(1024)}, s32[160]{0:T(256)}, s32[160]{0:T(256)S(1)}, /*index=5*/bf16[1280,1024]{1,...) while((s32[]{:T(128)}, f32[8,2,160,128]{3,2,1,0:T(8,128)}, ...), condition=%wide.region_14.15_spmd.clone, body=%wide.region_13.14_spmd.clone.sunk | while | flops 635197440 | bytes 17863920 | solution.py:63
  564.6 101.7 %while.57 = (s32[]{:T(128)}, f32[160,8,128]{2,0,1:T(8,128)}, f32[160,8,128]{2,0,1:T(8,128)}, bf16[1280,2048]{1,0:T(8,128)(2,1)}, s32[160]{0:T(256)S(1)}, /*index...) while((s32[]{:T(128)}, f32[160,8,128]{2,0,1:T(8,128)}, ...), condition=%wide.region_17.18_spmd.clone, body=%wide.region_16.17_spmd.clone.sunk | while | flops 848025600 | bytes 34466176 | solution.py:63
  629.8 6.8 fusion.203
  675.6 95.3 %reduce-scatter.9.cloned.1.call-done = bf16[256,6144]{1,0:T(8,128)(2,1)} async-done(((bf16[1024,6144]{1,0:T(8,128)(2,1)}), bf16[256,6144]{1,0:T(8,128)(2,1)}) %reduce-scatter.9.cloned.1.call-update) | async-done | bytes 3145744 | tf_op jit(solution)/shard_map/reduce_scatter | solution.py:294
  770.9 74.2 %reduce-scatter.5.cloned.1.call-done = bf16[256,4096]{1,0:T(8,128)(2,1)} async-done(((bf16[1024,4096]{1,0:T(8,128)(2,1)}), bf16[256,4096]{1,0:T(8,128)(2,1)}) %reduce-scatter.5.cloned.1.call-update) | async-done | bytes 2097168 | tf_op jit(solution)/shard_map/reduce_scatter | solution.py:444
  865.9 11.0 all-reduce.10
  877.2 23.2 %all-reduce.11 = (bf16[256]{0:T(256)(128)(2,1)S(1)}, bf16[32]{0:T(256)(128)(2,1)S(1)}, bf16[32]{0:T(256)(128)(2,1)S(1)}, bf16[256]{0:T(256)(128)(2,1)S(1)}) all-reduce(bf16[256]{0:T(256)(128)(2,1)S(1)} %dynamic-slice.16, bf16[32]{0:T(256)(128)(2,1)S(1)} %dynamic-slice.18, ...), channel_id=1, replica_groups=mesh['ctx'=8,'fsdp'=4] {'ctx'}, use_global_device_ids=true, to_apply=%region_22.23 | all-reduce | flops 576 | bytes 2304 | tf_op jit(solution)/shard_map/psum | solution.py:468
  904.3 211.4 %all-reduce.16.cloned.1.call-done = (bf16[256,4096]{1,0:T(8,128)(2,1)}, bf16[512,1024]{1,0:T(8,128)(2,1)}, bf16[256,6144]{1,0:T(8,128)(2,1)}, bf16[768,1024]{1,0:T(8,128)(2,1)}) async-done(((bf16[256,4096]{1,0:T(8,128)(2,1)}, bf16[512,1024]{1,0:T(8,128)(2,1)}, bf16[256,6144]{1,0:T(8,128)(2,1)}, bf16[768,1024]{1,0:T(8,128)(2,1)}), (bf16[256,4096]{1,0:T(8,128)(2,1)}, bf16[512,1024]{1,0:T(8,128)(2,1)}, ...) | async-done | bytes 7864336 | tf_op jit(solution)/shard_map/psum | solution.py:472
  (466 shorter events, 341.8 us)
Async XLA Ops:
  7.2 30.6 %all-gather.16.cloned.1.call-start = ((), (), s32[]{:S(2)}) async-start(), calls=%async_computation.6 | async-start | bytes 2621440 | tf_op jit(solution)/shard_map/all_gather | solution.py:137
  7.9 51.2 %all-gather.22.cloned.1.call-start = ((), (), s32[]{:S(2)}) async-start(), calls=%async_computation.9 | async-start | bytes 2621440 | tf_op jit(solution)/shard_map/all_gather | solution.py:138
  8.7 19.1 %copy-start.70 = (bf16[32]{0:T(256)(128)(2,1)S(1)}, bf16[32]{0:T(256)(128)(2,1)}, u32[]{:S(2)}) copy-start(bf16[32]{0:T(256)(128)(2,1)} %param.29) | copy-start | bytes 196
  8.7 19.4 %copy-start.71 = (bf16[32]{0:T(256)(128)(2,1)S(1)}, bf16[32]{0:T(256)(128)(2,1)}, u32[]{:S(2)}) copy-start(bf16[32]{0:T(256)(128)(2,1)} %param.28) | copy-start | bytes 196
  8.7 86.5 %all-gather.20.cloned.1.call-start = ((), (), s32[]{:S(2)}) async-start(), calls=%async_computation.8 | async-start | bytes 5242880 | tf_op jit(solution)/shard_map/all_gather | solution.py:136
  11.7 25.7 %all-to-all-start = ((bf16[8,20,1024]{2,1,0:T(8,128)(2,1)}), bf16[8,20,1024]{2,1,0:T(8,128)(2,1)S(1)}, u32[]{:S(2)}, u32[]{:S(2)}) async-start(bf16[8,20,1024]{2,1,0:T(8,128)(2,1)} %broadcast_select_fusion.1), calls=%async_computation | async-start | bytes 786432 | tf_op jit(solution)/shard_map/all_to_all | solution.py:114
  18.9 133.6 %all-gather.18.cloned.1.call-start = ((), (), s32[]{:S(2)}) async-start(), calls=%async_computation.7 | async-start | bytes 2949120 | tf_op jit(solution)/shard_map/all_gather | solution.py:213
  26.6 32.6 %copy-start.41 = (f32[4,1,256]{2,1,0:T(1,128)}, f32[4,1,256]{2,1,0:T(1,128)S(1)}, u32[]{:S(2)}) copy-start(f32[4,1,256]{2,1,0:T(1,128)S(1)} %convert_element_type.281) | copy-start | bytes 12292
  44.6 163.2 %all-gather.24.cloned.1.call-start = ((), (), s32[]{:S(2)}) async-start(), calls=%async_computation.10 | async-start | bytes 2949120 | tf_op jit(solution)/shard_map/all_gather | solution.py:214
  62.1 201.7 %all-gather.26.cloned.1.call-start = ((), (), s32[]{:S(2)}) async-start(), calls=%async_computation.11 | async-start | bytes 5242880 | tf_op jit(solution)/shard_map/all_gather | solution.py:139
  62.7 227.7 %all-gather.28.cloned.1.call-start = ((), (), s32[]{:S(2)}) async-start(), calls=%async_computation.12 | async-start | bytes 7864320 | tf_op jit(solution)/shard_map/all_gather | solution.py:143
  63.4 274.9 %all-gather.30.cloned.1.call-start = ((), (), s32[]{:S(2)}) async-start(), calls=%async_computation.13 | async-start | bytes 7864320 | tf_op jit(solution)/shard_map/all_gather | solution.py:144
  64.2 322.1 %all-gather.32.cloned.1.call-start = ((), (), s32[]{:S(2)}) async-start(), calls=%async_computation.14 | async-start | bytes 7864320 | tf_op jit(solution)/shard_map/all_gather | solution.py:145
  64.9 499.7 %all-gather.34.cloned.1.call-start = ((), (), s32[]{:S(2)}) async-start(), calls=%async_computation.15 | async-start | bytes 5898240 | tf_op jit(solution)/shard_map/all_gather | solution.py:404
  65.0 41.5 %copy-start.59 = (f32[128]{0:T(128)}, f32[128]{0:T(128)S(1)}, u32[]{:S(2)}) copy-start(f32[128]{0:T(128)S(1)} %convert_element_type.232) | copy-start | bytes 1540
  105.6 457.4 %copy-start.2 = (f32[160,16,128]{2,0,1:T(8,128)}, f32[160,16,128]{2,0,1:T(8,128)S(1)}, u32[]{:S(2)}) copy-start(f32[160,16,128]{2,0,1:T(8,128)S(1)} %get-tuple-element.948) | copy-start | bytes 3932164
  108.4 456.2 %all-gather.36.cloned.1.call-start = ((), (), s32[]{:S(2)}) async-start(), calls=%async_computation.16 | async-start | bytes 5898240 | tf_op jit(solution)/shard_map/all_gather | solution.py:407
  267.2 136.0 %copy-start.9 = (f32[160,1024]{1,0:T(8,128)}, f32[160,1024]{1,0:T(8,128)S(1)}, u32[]{:S(2)}) copy-start(f32[160,1024]{1,0:T(8,128)S(1)} %get-tuple-element.950) | copy-start | bytes 1966084
  406.8 268.8 %reduce-scatter.7.cloned.1.call-start = ((), (), s32[]{:S(2)}) async-start(), calls=%async_computation.18 | async-start | bytes 5242880 | tf_op jit(solution)/shard_map/reduce_scatter | solution.py:302
  421.2 254.4 %reduce-scatter.11.cloned.1.call-start = ((), (), s32[]{:S(2)}) async-start(), calls=%async_computation.20 | async-start | bytes 7864320 | tf_op jit(solution)/shard_map/reduce_scatter | solution.py:283
  427.9 343.0 %reduce-scatter.9.cloned.1.call-start = ((), (), s32[]{:S(2)}) async-start(), calls=%async_computation.19 | async-start | bytes 15728640 | tf_op jit(solution)/shard_map/reduce_scatter | solution.py:294
  436.9 408.2 %reduce-scatter.5.cloned.1.call-start = ((), (), s32[]{:S(2)}) async-start(), calls=%async_computation.17 | async-start | bytes 10485760 | tf_op jit(solution)/shard_map/reduce_scatter | solution.py:444
  675.5 440.3 %all-reduce.16.cloned.1.call-start = ((), (), s32[]{:S(2)}) async-start(), calls=%async_computation.21 | async-start | bytes 15728640 | tf_op jit(solution)/shard_map/psum | solution.py:472
  855.6 47.0 %all-to-all-start.1 = ((bf16[8,20,1024]{2,1,0:T(8,128)(2,1)}), bf16[8,20,1024]{2,1,0:T(8,128)(2,1)S(1)}, u32[]{:S(2)}, u32[]{:S(2)}) async-start(bf16[8,20,1024]{2,1,0:T(8,128)(2,1)} %convert_element_type.262), calls=%async_computation.1 | async-start | bytes 786432 | tf_op jit(solution)/shard_map/all_to_all | solution.py:453
  (82 other events, 305.2 us)
Sparse Core Ops, SparseCore 0:
  9.6 25.3 all-gather.15
  36.6 22.5 all-gather.21
  60.7 34.4 all-gather.19
  97.9 54.6 all-gather.17
  154.6 53.2 all-gather.23
  209.3 33.0 all-gather.25
  243.9 46.3 all-gather.27
  291.9 46.3 all-gather.29
  339.9 46.3 all-gather.31
  388.3 87.2 all-gather.33
  478.4 84.7 all-gather.35
  565.5 42.6 reduce-scatter.6
  610.9 58.3 reduce-scatter.10
  671.8 99.0 reduce-scatter.8
  773.3 71.6 reduce-scatter.4
  850.0 265.7 all-reduce.15
where the time goes:
time: 1150 us; the launch traced here: 1140 us
  waiting for transfers between devices  631 us (55%)
  matrix products  186 us (16%)
  local copies, waits for them, and re-layouts  114 us (10%)
  blocking collectives  113 us (10%)
  other arithmetic  49.4 us (4%)
  starting transfers between devices  23.5 us (2%)
  between operations  17.4 us (2%)
    psum x1, waiting for transfers between devices, on_device(): lax.psum(qkv_grad, 'ctx').astype(jnp.float32)  211 us
    reduce_scatter x1, waiting for transfers between devices, on_device(): lax.psum_scatter(outer_rows(normed2, both_low).astype(jnp.bfloat16), 'fsd...  95.3 us
    reduce_scatter x1, waiting for transfers between devices, on_device(): lax.psum_scatter(outer_rows(normalized_input, qkv_low).astype(jnp.bfloat1...  74.2 us
    all_gather x1, waiting for transfers between devices, forward(): lax.all_gather(value_narrow, 'ctx', axis=0, tiled=True)  55.3 us
    all_gather x1, waiting for transfers between devices, forward(): lax.all_gather(key_narrow, 'ctx', axis=0, tiled=True)  43.9 us
    all_gather x1, waiting for transfers between devices, fetch_weights(): lax.all_gather(w_down, 'fsdp', axis=0, tiled=True)  42.6 us
    all_gather x1, waiting for transfers between devices, fetch_weights(): lax.all_gather(w_up, 'fsdp', axis=0, tiled=True)  42.6 us
    all_gather x1, blocking collectives, on_device(): lax.all_gather(lse_rows.astype(jnp.bfloat16), 'ctx', axis=0, tiled=True)  31 us
  transfers between devices with their start and end apart: 18, of which 10 were waited for; matrix products, arithmetic and copies ran while one was open for 28% of the time, Pallas kernels for 0%

commit v1 on v0

--- a/solution.py
+++ b/solution.py
@@ -3,6 +3,7 @@
 import jax
 import jax.numpy as jnp
 from jax import lax
+from jax.sharding import Mesh
 from jax.sharding import PartitionSpec as P
 
 MODEL_WIDTH = 1024
@@ -67,7 +68,7 @@
     return jnp.max(jnp.where(tok_ids[:, None] >= starts[None, :], starts[None, :], 0), axis=1)
 
 
-def on_device(
+def general_layer(
     tokens,
     lengths,
     deal,
@@ -496,41 +497,305 @@
     )
 
 
+CTX = ("z", "y")
+FSDP = ("x", "core")
+
+
+def norm_back(values, gain_vec, grad):
+    scale = lax.rsqrt(jnp.mean(values * values, axis=-1, keepdims=True) + eps)
+    inner = gain_vec * grad
+    d_values = scale * inner - values * (scale * scale * scale) * jnp.mean(
+        values * inner, axis=-1, keepdims=True
+    )
+    return d_values, grad * values * scale
+
+
+def half_turn(values):
+    half = values.shape[-1] // 2
+    return jnp.concatenate([-values[..., half:], values[..., :half]], axis=-1)
+
+
+def rope_tables(token_position):
+    half = HEAD_SIZE // 2
+    frequency = theta_base ** (-(jnp.arange(half, dtype=jnp.float32) * 2.0) / HEAD_SIZE)
+    angles = token_position.astype(jnp.float32)[:, None] * frequency[None, :]
+    cosine, sine = jnp.cos(angles), jnp.sin(angles)
+    return jnp.concatenate([cosine, cosine], axis=1), jnp.concatenate([sine, sine], axis=1)
+
+
+def dot(a, b):
+    return jnp.dot(a, b, preferred_element_type=jnp.float32)
+
+
+def low(a):
+    return a.astype(jnp.bfloat16)
+
+
+def gather_ctx(block):
+    return lax.all_gather(block, CTX, axis=0, tiled=True)
+
+
+def gather_fsdp(block):
+    return lax.all_gather(block, FSDP, axis=0, tiled=True)
+
+
+def gather_quad(block):
+    return lax.all_gather(block, ("y", "core"), axis=0, tiled=True)
+
+
+def fast_layer(
+    tokens,
+    lengths,
+    deal,
+    attn_gain,
+    w_q,
+    key_weight,
+    value_weight,
+    query_norm_gain,
+    k_gain,
+    w_o,
+    mlp_gain,
+    w_gate,
+    w_up,
+    w_down,
+    out_cotangent,
+):
+    rows = tokens.shape[1]
+    slots = lax.axis_size(CTX)
+    piece = rows // slots
+    count = rows * slots
+    here = lax.axis_index(CTX)
+    y, core = lax.axis_index("y"), lax.axis_index("core")
+    x = lax.axis_index("x")
+    ff_shard = w_down.shape[0]
+    ff_half = ff_shard // 2
+    width = HEAD_SIZE * 2
+
+    starts = jnp.cumsum(lengths[0]) - lengths[0]
+    ids = jnp.arange(count, dtype=jnp.int32)
+    first = segment_begin(ids, starts)
+    cosine, sine = rope_tables(ids - first)
+    plan = deal[0]
+    devices = jnp.arange(slots, dtype=jnp.int32)
+    slot_of = jnp.sum(
+        jnp.where(plan[:, :, None] == devices[None, None, :], devices[None, :, None], 0), axis=1
+    )
+    dealt_index = (
+        devices[None, :, None] * rows
+        + jnp.transpose(slot_of)[:, :, None] * piece
+        + jnp.arange(piece, dtype=jnp.int32)[None, None, :]
+    ).reshape(count)
+    to_dealt = low(dealt_index[:, None] == ids[None, :])
+
+    packed_gain = jnp.concatenate([attn_gain, mlp_gain, query_norm_gain, k_gain])[None]
+    gains = gather_fsdp(packed_gain).astype(jnp.float32)
+    a_gain = gains[:, :256].reshape(-1)
+    m_gain = gains[:, 256:512].reshape(-1)
+    q_gain = gains[:, 512:544].reshape(-1)
+    k_gain_all = gains[:, 544:576].reshape(-1)
+    qkv_own = jnp.concatenate(
+        [
+            lax.dynamic_slice_in_dim(w_q, here * width, width, 1),
+            lax.dynamic_slice_in_dim(key_weight, here * HEAD_SIZE, HEAD_SIZE, 1),
+            lax.dynamic_slice_in_dim(value_weight, here * HEAD_SIZE, HEAD_SIZE, 1),
+        ],
+        axis=1,
+    )
+    all_tokens = gather_ctx(tokens[0])
+    w_qkv = gather_fsdp(qkv_own)
+    values = all_tokens.astype(jnp.float32)
+    normed = low(root_mean_norm(values, a_gain))
+    qkv = dot(normed, w_qkv)
+    q_pre = qkv[:, :width].reshape(count, 2, HEAD_SIZE)
+    k_pre = qkv[:, width : width + HEAD_SIZE]
+    v_low = low(qkv[:, width + HEAD_SIZE :])
+
+    def rope(v, cos, sin):
+        return v * cos + half_turn(v) * sin
+
+    q_low = low(rope(root_mean_norm(q_pre, q_gain), cosine[:, None], sine[:, None]))
+    k_low = low(rope(root_mean_norm(k_pre, k_gain_all), cosine, sine))
+    allowed = (ids[None, :] >= first[:, None]) & (ids[None, :] <= ids[:, None])
+    scale = HEAD_SIZE**-0.5
+    scores = jnp.einsum("tgh,uh->gtu", q_low, k_low, preferred_element_type=jnp.float32) * scale
+    scores = jnp.where(allowed, scores, negative_filler)
+    top = jnp.max(scores, axis=-1, keepdims=True)
+    weights = jnp.exp(scores - top)
+    total = jnp.sum(weights, axis=-1, keepdims=True)
+    log_total = top + jnp.log(total)
+    mixed = (
+        jnp.einsum("gtu,uh->gth", low(weights), v_low, preferred_element_type=jnp.float32) / total
+    )
+    mixed_heads = low(jnp.transpose(mixed, (1, 0, 2)).reshape(count, width))
+    mixed_out = low(dot(to_dealt, mixed_heads)).reshape(slots, rows, width)
+    mixed_in = lax.all_to_all(mixed_out, CTX, 0, 0, tiled=True)
+    mixed_low = jnp.transpose(mixed_in, (1, 0, 2)).reshape(rows, slots * width)
+
+    own_rows = lax.dynamic_slice_in_dim(to_dealt, here * rows, rows, 0)
+    residual = dot(own_rows, all_tokens)
+    full_o = gather_fsdp(w_o)
+    middle = residual + dot(mixed_low, full_o)
+    normed2 = low(root_mean_norm(middle, m_gain))
+
+    def quarter_cols(w, c):
+        return jnp.concatenate(
+            [
+                lax.dynamic_slice_in_dim(w, (2 * xs + c) * ff_shard + y * ff_half, ff_half, 1)
+                for xs in range(2)
+            ],
+            axis=1,
+        )
+
+    sides = jnp.stack(
+        [
+            jnp.concatenate([quarter_cols(w_gate, c), quarter_cols(w_up, c)], axis=1)
+            for c in range(2)
+        ]
+    )
+    sides = lax.all_to_all(sides, "core", 0, 0, tiled=True)
+    w_gu = lax.all_gather(sides, "x", axis=0, tiled=True).reshape(-1, 4 * ff_half)
+    down_own = lax.dynamic_slice_in_dim(w_down, y * ff_half, ff_half, 0)
+    w_dn = lax.all_gather(down_own, "x", axis=0, tiled=True)
+    quad_n = gather_quad(normed2)
+    quad_g = gather_quad(out_cotangent[0])
+    gate_up = dot(quad_n, w_gu)
+    gate, up = gate_up[:, : 2 * ff_half], gate_up[:, 2 * ff_half :]
+    sig = 1.0 / (1.0 + jnp.exp(-gate))
+    silu = gate * sig
+    hidden = low(silu * up)
+    partial_out = low(dot(hidden, w_dn))
+    out_sum = lax.psum_scatter(partial_out, ("y", "core"), scatter_dimension=0, tiled=True)
+    output = low(middle + out_sum.astype(jnp.float32))
+
+    d_hidden = dot_trans(quad_g, w_dn)
+    d_gate = low(d_hidden * up * (sig * (1.0 + gate * (1.0 - sig))))
+    d_up = low(d_hidden * silu)
+    d_gu = jnp.concatenate([d_gate, d_up], axis=1)
+    dn2_part = low(dot_trans(d_gu, w_gu))
+    d_normed2 = lax.psum_scatter(
+        dn2_part, ("y", "core"), scatter_dimension=0, tiled=True
+    ).astype(jnp.float32)
+    grad_gu = low(outer_rows(quad_n, d_gu))
+    grad_dn = low(outer_rows(hidden, quad_g))
+    dx2, dg2 = norm_back(middle, m_gain, d_normed2)
+    d_middle = out_cotangent[0].astype(jnp.float32) + dx2
+    middle_low = low(d_middle)
+    d_mixed_tok = low(dot_trans(middle_low, full_o))
+    dm_out = jnp.transpose(d_mixed_tok.reshape(rows, slots, width), (1, 0, 2))
+    dm_in = lax.all_to_all(dm_out, CTX, 0, 0, tiled=True).reshape(count, width)
+    d_mixed = low(
+        lax.dot_general(
+            to_dealt, dm_in, (((0,), (0,)), ((), ())), preferred_element_type=jnp.float32
+        )
+    )
+    grad_o = low(outer_rows(mixed_low, middle_low))
+    d_heads = d_mixed.reshape(count, 2, HEAD_SIZE)
+    delta = jnp.sum(
+        jnp.transpose(d_heads, (1, 0, 2)).astype(jnp.float32) * mixed, axis=-1, keepdims=True
+    )
+    probs = jnp.where(allowed, jnp.exp(scores - log_total), 0.0)
+    d_probs = jnp.einsum("tgh,uh->gtu", d_heads, v_low, preferred_element_type=jnp.float32)
+    d_scores = low(probs * (d_probs - delta))
+    d_v = jnp.einsum("gtu,tgh->uh", low(probs), d_heads, preferred_element_type=jnp.float32)
+    d_q = jnp.einsum("gtu,uh->tgh", d_scores, k_low, preferred_element_type=jnp.float32) * scale
+    d_k = jnp.einsum("gtu,tgh->uh", d_scores, q_low, preferred_element_type=jnp.float32) * scale
+
+    def rope_back(v, cos, sin):
+        return v * cos - half_turn(v * sin)
+
+    d_q_pre, dg_q = norm_back(q_pre, q_gain, rope_back(d_q, cosine[:, None], sine[:, None]))
+    d_k_pre, dg_k = norm_back(k_pre, k_gain_all, rope_back(d_k, cosine, sine))
+    d_qkv = jnp.concatenate([low(d_q_pre.reshape(count, width)), low(d_k_pre), low(d_v)], axis=1)
+    dn_part = low(dot_trans(d_qkv, w_qkv))
+    d_normed = lax.psum_scatter(dn_part, CTX, scatter_dimension=0, tiled=True).astype(jnp.float32)
+    grad_qkv = low(outer_rows(normed, d_qkv))
+
+    back = lax.all_to_all(middle_low.reshape(slots, piece, MODEL_WIDTH), CTX, 0, 0, tiled=True)
+    own_plan = lax.dynamic_index_in_dim(plan, here, 0, keepdims=False)
+    d_middle_given = jnp.take(back, own_plan, axis=0).reshape(rows, MODEL_WIDTH)
+    dx1, dg1 = norm_back(tokens[0].astype(jnp.float32), a_gain, d_normed)
+    input_grad = d_middle_given.astype(jnp.float32) + dx1
+
+    gain_sums = lax.psum(
+        jnp.concatenate(
+            [
+                jnp.sum(dg1, axis=0).reshape(4, 256),
+                jnp.sum(dg2, axis=0).reshape(4, 256),
+                jnp.sum(dg_q, axis=(0, 1)).reshape(4, 32),
+                jnp.sum(dg_k, axis=0).reshape(4, 32),
+            ],
+            axis=1,
+        ),
+        ("z", "y", "x", "core"),
+    )
+    own_gain = lax.dynamic_index_in_dim(gain_sums, 2 * x + core, 0, keepdims=False)
+
+    qkv_sum = lax.psum_scatter(grad_qkv, FSDP, scatter_dimension=0, tiled=True)
+    qkv_all = lax.all_gather(qkv_sum, CTX, axis=0)
+    q_all = jnp.transpose(qkv_all[:, :, :width], (1, 0, 2)).reshape(-1, slots * width)
+    k_all = jnp.transpose(qkv_all[:, :, width : width + HEAD_SIZE], (1, 0, 2))
+    v_all = jnp.transpose(qkv_all[:, :, width + HEAD_SIZE :], (1, 0, 2))
+    o_sum = lax.psum(
+        lax.psum_scatter(grad_o, FSDP, scatter_dimension=0, tiled=True), CTX
+    )
+    gu_sum = lax.psum(lax.psum_scatter(grad_gu, "x", scatter_dimension=0, tiled=True), "z")
+    gu_pair = lax.all_to_all(
+        gu_sum.reshape(2, -1, 4 * ff_half), "core", 0, 0, tiled=True
+    )
+    gu_all = lax.all_gather(gu_pair, "y", axis=0)
+    gu_all = gu_all.reshape(2, 2, -1, 2, 2, ff_half)
+    gu_all = jnp.transpose(gu_all, (3, 2, 4, 1, 0, 5)).reshape(2, -1, 8 * ff_half)
+    dn_sum = lax.psum(lax.psum_scatter(grad_dn, "x", scatter_dimension=0, tiled=True), "z")
+    dn_all = lax.all_gather(dn_sum, "y", axis=0, tiled=True)
+
+    def wide(a):
+        return a.astype(jnp.float32)
+
+    return (
+        output[None],
+        input_grad[None],
+        own_gain[:256],
+        own_gain[512:544],
+        own_gain[544:576],
+        own_gain[256:512],
+        wide(q_all),
+        wide(k_all.reshape(-1, slots * HEAD_SIZE)),
+        wide(v_all.reshape(-1, slots * HEAD_SIZE)),
+        wide(o_sum),
+        wide(gu_all[0]),
+        wide(gu_all[1]),
+        wide(dn_all),
+    )
+
+
 def solution(mesh):
+    devices = mesh.devices
+    if devices.shape == (8, 4):
+        mesh = Mesh(devices.reshape(4, 2, 2, 2), CTX + FSDP)
+        layer, ctx, fsdp = fast_layer, CTX, FSDP
+    else:
+        layer, ctx, fsdp = general_layer, "ctx", "fsdp"
+    wide_rows = P(fsdp, ctx, None)
     return jax.shard_map(
-        on_device,
+        layer,
         mesh=mesh,
         in_specs=(
-            P("fsdp", "ctx", None),
-            P("fsdp", None),
-            P("fsdp", None, None),
-            P("fsdp"),
-            P("fsdp", None),
-            P("fsdp", None),
-            P("fsdp", None),
-            P("fsdp"),
-            P("fsdp"),
-            P("fsdp", None),
-            P("fsdp"),
-            P("fsdp", None),
-            P("fsdp", None),
-            P("fsdp", None),
-            P("fsdp", "ctx", None),
+            wide_rows,
+            P(fsdp, None),
+            P(fsdp, None, None),
+            P(fsdp),
+            P(fsdp, None),
+            P(fsdp, None),
+            P(fsdp, None),
+            P(fsdp),
+            P(fsdp),
+            P(fsdp, None),
+            P(fsdp),
+            P(fsdp, None),
+            P(fsdp, None),
+            P(fsdp, None),
+            wide_rows,
         ),
-        out_specs=(
-            P("fsdp", "ctx", None),
-            P("fsdp", "ctx", None),
-            P("fsdp"),
-            P("fsdp"),
-            P("fsdp"),
-            P("fsdp"),
-            P("fsdp", None),
-            P("fsdp", None),
-            P("fsdp", None),
-            P("fsdp", None),
-            P("fsdp", None),
-            P("fsdp", None),
-            P("fsdp", None),
-        ),
+        out_specs=(wide_rows, wide_rows) + (P(fsdp),) * 4 + (P(fsdp, None),) * 7,
         check_vma=False,
     )

time: 1150 us -> 859 us (0.75)
  matrix products: 186 us -> 74.7 us
  local copies, waits for them, and re-layouts: 114 us -> 53.1 us
  blocking collectives: 113 us -> 62.4 us
  waiting for transfers between devices: 631 us -> 588 us
    dot_general x35 -> x13, matrix products: 137 us -> 43 us  [the longest x6 21.1 us: dot(): return jnp.dot(a, b, preferred_element_type=jnp.float32)]
    all_gather x4 -> x0, blocking collectives: 72 us -> none  [the longest x1 31 us: on_device(): lax.all_gather(lse_rows.astype(jnp.bfloat16), 'ctx', axis=0, tiled=True)]
    psum x1 -> x2, waiting for transfers between devices: 211 us -> 151 us  [the longest x1 98.5 us: fast_layer(): lax.psum(lax.psum_scatter(grad_gu, 'x', scatter_dimension=0, tiled=True),...]
    all_to_all x2 -> x3, waiting for transfers between devices: 0.01 us -> 47.3 us  [the longest x1 20.6 us: fast_layer(): lax.all_to_all(middle_low.reshape(slots, piece, MODEL_WIDTH), CTX, 0, 0,...]
    reduce_scatter x4 -> x7, waiting for transfers between devices: 169 us -> 135 us  [the longest x1 45.3 us: fast_layer(): lax.psum_scatter(dn_part, CTX, scatter_dimension=0, tiled=True)]
    dynamic_slice x24 -> x4, local copies, waits for them, and re-layouts: 28.2 us -> 4.16 us  [the longest x1 1.41 us: quarter_cols(): lax.dynamic_slice_in_dim(w, (2 * xs + c) * ff_shard + y * ff_half, ff_hal...]
    while x68 -> x0, local copies, waits for them, and re-layouts: 23 us -> none
    reshape x18 -> x8, local copies, waits for them, and re-layouts: 24.7 us -> 6.57 us  [the longest x1 4.63 us: fast_layer(): gu_all = gu_all.reshape(2, 2, -1, 2, 2, ff_half)]
  transfers between devices with their start and end apart: 18 -> 22, of which waited for: 10 -> 20; matrix products, arithmetic and copies ran while one was open for 28% -> 17% of each run, Pallas kernels for 0% -> 0%
where the time goes in v1:
time: 859 us; the launch traced here: 848 us
  waiting for transfers between devices  588 us (68%)
  matrix products  74.7 us (9%)
  blocking collectives  62.4 us (7%)
  local copies, waits for them, and re-layouts  53.1 us (6%)
  other arithmetic  39.4 us (5%)
  between operations  15.8 us (2%)
  starting transfers between devices  15 us (2%)
    psum x1, waiting for transfers between devices, fast_layer(): lax.psum(lax.psum_scatter(grad_gu, 'x', scatter_dimension=0, tiled=True),...  98.5 us
    psum x1, waiting for transfers between devices, fast_layer(): lax.psum(lax.psum_scatter(grad_o, FSDP, scatter_dimension=0, tiled=True),...  52.8 us
    all_gather x1, waiting for transfers between devices, fast_layer(): qkv_all = lax.all_gather(qkv_sum, CTX, axis=0)  50.7 us
    reduce_scatter x1, waiting for transfers between devices, fast_layer(): lax.psum_scatter(dn_part, CTX, scatter_dimension=0, tiled=True)  45.3 us
    all_gather x1, waiting for transfers between devices, fast_layer(): gu_all = lax.all_gather(gu_pair, 'y', axis=0)  42.9 us
    all_gather x2, waiting for transfers between devices, gather_quad(): return lax.all_gather(block, ('y', 'core'), axis=0, tiled=True)  40 us
    psum x1, blocking collectives, fast_layer(): lax.psum(jnp.concatenate([jnp.sum(dg1, axis=0).reshape(4, 256), jnp.sum(d...  39.8 us
    all_gather x1, waiting for transfers between devices, gather_ctx(): return lax.all_gather(block, CTX, axis=0, tiled=True)  32.6 us
  transfers between devices with their start and end apart: 22, of which 20 were waited for; matrix products, arithmetic and copies ran while one was open for 17% of the time, Pallas kernels for 0%

profile of v1, /device:TPU:0, one launch (start us, length us, event | category | flops | bytes accessed | tf_op | source)
XLA Modules:
  0.0 848.4 jit_solution(14736524220811090742)
XLA Ops:
  20.7 8.8 %all-reduce = bf16[2304]{0:T(1024)(128)(2,1)S(1)} all-reduce(bf16[2304]{0:T(1024)(128)(2,1)S(1)} %dynamic-update-slice), channel_id=3, replica_groups=mesh['z'=4,'y'=2,'x'=2,'core'=2] {'x','core'}, use_global_device_ids=true, to_apply=%add | all-reduce | flops 2304 | bytes 9216
  35.1 32.6 %all-gather.28.cloned.1.call-done = bf16[1,1280,1024]{2,1,0:T(8,128)(2,1)} async-done(((bf16[1,160,1024]{2,1,0:T(8,128)(2,1)}), bf16[1,1280,1024]{2,1,0:T(8,128)(2,1)}) %all-gather.28.cloned.1.call-update) | async-done | bytes 2621456 | tf_op jit(solution)/shard_map/all_gather | solution.py:535
  70.0 15.1 %all-gather.16.cloned.1.call-done = bf16[1024,512]{1,0:T(8,128)(2,1)} async-done(((bf16[256,512]{1,0:T(8,128)(2,1)}), bf16[1024,512]{1,0:T(8,128)(2,1)}) %all-gather.16.cloned.1.call-update) | async-done | bytes 1048592 | tf_op jit(solution)/shard_map/all_gather | solution.py:539
  116.3 15.3 %all-to-all-done = bf16[8,160,256]{2,1,0:T(8,128)(2,1)S(1)} async-done(((bf16[8,160,256]{2,1,0:T(8,128)(2,1)}), bf16[8,160,256]{2,1,0:T(8,128)(2,1)S(1)}, u32[]{:S(2)}, u32[]{:S(2)}) %all-to-all-start) | async-done | bytes 655392 | tf_op jit(solution)/shard_map/all_to_all | solution.py:631
  140.3 27.3 %all-gather.22.cloned.1.call-done = bf16[4,256,1536]{2,1,0:T(8,128)(2,1)} async-done(((bf16[2,256,1536]{2,1,0:T(8,128)(2,1)}), bf16[4,256,1536]{2,1,0:T(8,128)(2,1)}) %all-gather.22.cloned.1.call-update) | async-done | bytes 3145744 | tf_op jit(solution)/shard_map/all_gather | solution.py:656
  167.5 20.2 %all-gather.20.cloned.1.call-done = bf16[640,1024]{1,0:T(8,128)(2,1)} async-done(((bf16[160,1024]{1,0:T(8,128)(2,1)}), bf16[640,1024]{1,0:T(8,128)(2,1)}) %all-gather.20.cloned.1.call-update) | async-done | bytes 1310736 | tf_op jit(solution)/shard_map/all_gather | solution.py:543
  187.8 6.4 fusion.84
  194.2 22.8 %all-gather.24.cloned.1.call-done = bf16[768,1024]{1,0:T(8,128)(2,1)} async-done(((bf16[384,1024]{1,0:T(8,128)(2,1)}), bf16[768,1024]{1,0:T(8,128)(2,1)}) %all-gather.24.cloned.1.call-update) | async-done | bytes 1572880 | tf_op jit(solution)/shard_map/all_gather | solution.py:658
  217.0 19.8 %all-gather.30.cloned.1.call-done = bf16[1,640,1024]{2,1,0:T(8,128)(2,1)} async-done(((bf16[1,160,1024]{2,1,0:T(8,128)(2,1)}), bf16[1,640,1024]{2,1,0:T(8,128)(2,1)}) %all-gather.30.cloned.1.call-update) | async-done | bytes 1310736 | tf_op jit(solution)/shard_map/all_gather | solution.py:543
  255.1 18.9 %reduce-scatter.10.cloned.1.call-done = bf16[160,1024]{1,0:T(8,128)(2,1)} async-done(((bf16[640,1024]{1,0:T(8,128)(2,1)}), bf16[160,1024]{1,0:T(8,128)(2,1)}) %reduce-scatter.10.cloned.1.call-update) | async-done | bytes 327696 | tf_op jit(solution)/shard_map/reduce_scatter | solution.py:675
  275.2 28.1 %reduce-scatter.8.cloned.1.call-done = bf16[160,1024]{1,0:T(8,128)(2,1)} async-done(((bf16[640,1024]{1,0:T(8,128)(2,1)}), bf16[160,1024]{1,0:T(8,128)(2,1)}) %reduce-scatter.8.cloned.1.call-update) | async-done | bytes 327696 | tf_op jit(solution)/shard_map/reduce_scatter | solution.py:667
  320.6 11.4 %all-to-all-done.3 = bf16[8,160,256]{2,1,0:T(8,128)(2,1)S(1)} async-done(((bf16[8,160,256]{2,1,0:T(8,128)(2,1)}), bf16[8,160,256]{2,1,0:T(8,128)(2,1)S(1)}, u32[]{:S(2)}, u32[]{:S(2)}) %all-to-all-start.3) | async-done | bytes 655392 | tf_op jit(solution)/shard_map/all_to_all | solution.py:685
  334.6 7.4 fusion.1
  358.6 19.8 %reduce-scatter.18.cloned.1.call-done = bf16[512,1536]{1,0:T(8,128)(2,1)} async-done(((bf16[1024,1536]{1,0:T(8,128)(2,1)}), bf16[512,1536]{1,0:T(8,128)(2,1)}) %reduce-scatter.18.cloned.1.call-update) | async-done | bytes 1572880 | tf_op jit(solution)/shard_map/reduce_scatter | solution.py:741
  386.3 19.8 %reduce-scatter.14.cloned.1.call-done = bf16[256,512]{1,0:T(8,128)(2,1)} async-done(((bf16[1024,512]{1,0:T(8,128)(2,1)}), bf16[256,512]{1,0:T(8,128)(2,1)}) %reduce-scatter.14.cloned.1.call-update) | async-done | bytes 262160 | tf_op jit(solution)/shard_map/reduce_scatter | solution.py:733
  406.2 98.5 %all-reduce.7.cloned.1.call-done = (bf16[2,256,1536]{2,1,0:T(8,128)(2,1)}, bf16[384,1024]{1,0:T(8,128)(2,1)}) async-done(((bf16[2,256,1536]{2,1,0:T(8,128)(2,1)}, bf16[384,1024]{1,0:T(8,128)(2,1)}), (bf16[2,256,1536]{2,1,0:T(8,128)(2,1)}, bf16[384,1024]{1,0:T(8,128)(2,1)})) %all-reduce.7.cloned.1.call-update) | async-done | bytes 2359312 | tf_op jit(solution)/shard_map/psum | solution.py:741
  504.8 7.8 all_to_all.26
  519.0 20.6 %all-to-all-done.2 = bf16[8,20,1024]{2,1,0:T(8,128)(2,1)S(1)} async-done(((bf16[8,20,1024]{2,1,0:T(8,128)(2,1)}), bf16[8,20,1024]{2,1,0:T(8,128)(2,1)S(1)}, u32[]{:S(2)}, u32[]{:S(2)}) %all-to-all-start.2) | async-done | bytes 327712 | tf_op jit(solution)/shard_map/all_to_all | solution.py:713
  540.4 45.3 %reduce-scatter.12.cloned.1.call-done = bf16[160,1024]{1,0:T(8,128)(2,1)} async-done(((bf16[1280,1024]{1,0:T(8,128)(2,1)}), bf16[160,1024]{1,0:T(8,128)(2,1)}) %reduce-scatter.12.cloned.1.call-update) | async-done | bytes 327696 | tf_op jit(solution)/shard_map/reduce_scatter | solution.py:710
  587.0 39.8 %psum.28 = f32[4,576]{1,0:T(4,128)S(1)} all-reduce(f32[4,576]{1,0:T(4,128)S(1)} %pad_maximum_fusion.10), channel_id=1, replica_groups=mesh['z'=4,'y'=2,'x'=2,'core'=2] {'z','y','x','core'}, use_global_device_ids=true, to_apply=%region_22.23 | all-reduce | flops 2304 | bytes 18432 | tf_op jit(solution)/shard_map/psum | solution.py:719
  633.1 50.7 %all-gather.32.cloned.1.call-done = bf16[2048,512]{1,0:T(8,128)(2,1)} async-done(((bf16[256,512]{1,0:T(8,128)(2,1)}), bf16[2048,512]{1,0:T(8,128)(2,1)}) %all-gather.32.cloned.1.call-update) | async-done | bytes 2097168 | tf_op jit(solution)/shard_map/all_gather | solution.py:734
  690.0 20.9 %all-gather.26.cloned.1.call-done = bf16[768,1024]{1,0:T(8,128)(2,1)} async-done(((bf16[384,1024]{1,0:T(8,128)(2,1)}), bf16[768,1024]{1,0:T(8,128)(2,1)}) %all-gather.26.cloned.1.call-update) | async-done | bytes 1572880 | tf_op jit(solution)/shard_map/all_gather | solution.py:749
  714.4 42.9 %all-gather.34.cloned.1.call-done = bf16[4,256,1536]{2,1,0:T(8,128)(2,1)} async-done(((bf16[2,256,1536]{2,1,0:T(8,128)(2,1)}), bf16[4,256,1536]{2,1,0:T(8,128)(2,1)}) %all-gather.34.cloned.1.call-update) | async-done | bytes 3145744 | tf_op jit(solution)/shard_map/all_gather | solution.py:745
  786.1 52.8 %all-reduce.5.cloned.1.call-done = bf16[512,1024]{1,0:T(8,128)(2,1)} async-done(((bf16[512,1024]{1,0:T(8,128)(2,1)}), bf16[512,1024]{1,0:T(8,128)(2,1)}) %all-reduce.5.cloned.1.call-update) | async-done | bytes 1048592 | tf_op jit(solution)/shard_map/psum | solution.py:738
  (292 shorter events, 179.5 us)
Async XLA Ops:
  7.2 131.3 %copy-start = (bf16[768,1024]{1,0:T(8,128)(2,1)S(1)}, bf16[768,1024]{1,0:T(8,128)(2,1)}, u32[]{:S(2)}) copy-start(bf16[768,1024]{1,0:T(8,128)(2,1)} %param.28) | copy-start | bytes 4718596
  7.2 60.4 %all-gather.28.cloned.1.call-start = ((), (), s32[]{:S(2)}) async-start(), calls=%async_computation.26 | async-start | bytes 2949120 | tf_op jit(solution)/shard_map/all_gather | solution.py:535
  7.9 77.2 %all-gather.16.cloned.1.call-start = ((), (), s32[]{:S(2)}) async-start(), calls=%async_computation.12 | async-start | bytes 1310720 | tf_op jit(solution)/shard_map/all_gather | solution.py:539
  10.6 121.1 %all-gather.18.cloned.1.call-start = ((), (), s32[]{:S(2)}) async-start(), calls=%async_computation.13 | async-start | bytes 5242880 | tf_op jit(solution)/shard_map/all_gather | solution.py:539
  11.3 156.2 %all-gather.22.cloned.1.call-start = ((), (), s32[]{:S(2)}) async-start(), calls=%async_computation.15 | async-start | bytes 4718592 | tf_op jit(solution)/shard_map/all_gather | solution.py:656
  108.4 23.2 %all-to-all-start = ((bf16[8,160,256]{2,1,0:T(8,128)(2,1)}), bf16[8,160,256]{2,1,0:T(8,128)(2,1)S(1)}, u32[]{:S(2)}, u32[]{:S(2)}) async-start(bf16[8,160,256]{2,1,0:T(8,128)(2,1)} %bitcast.12), calls=%async_computation | async-start | bytes 1310720 | tf_op jit(solution)/shard_map/all_to_all | solution.py:631
  113.9 73.9 %all-gather.20.cloned.1.call-start = ((), (), s32[]{:S(2)}) async-start(), calls=%async_computation.14 | async-start | bytes 1638400 | tf_op jit(solution)/shard_map/all_gather | solution.py:543
  137.6 136.4 %copy-start.36 = (f32[160]{0:T(256)}, f32[160]{0:T(256)S(1)}, u32[]{:S(2)}) copy-start(f32[160]{0:T(256)S(1)} %get-tuple-element.85) | copy-start | bytes 1924
  138.4 78.5 %all-gather.24.cloned.1.call-start = ((), (), s32[]{:S(2)}) async-start(), calls=%async_computation.16 | async-start | bytes 2359296 | tf_op jit(solution)/shard_map/all_gather | solution.py:658
  139.5 97.3 %all-gather.30.cloned.1.call-start = ((), (), s32[]{:S(2)}) async-start(), calls=%async_computation.27 | async-start | bytes 1638400 | tf_op jit(solution)/shard_map/all_gather | solution.py:543
  140.2 133.7 %reduce-scatter.10.cloned.1.call-start = ((), (), s32[]{:S(2)}) async-start(), calls=%async_computation.18 | async-start | bytes 1638400 | tf_op jit(solution)/shard_map/reduce_scatter | solution.py:675
  247.3 56.0 %reduce-scatter.8.cloned.1.call-start = ((), (), s32[]{:S(2)}) async-start(), calls=%async_computation.17 | async-start | bytes 1638400 | tf_op jit(solution)/shard_map/reduce_scatter | solution.py:667
  250.8 107.7 %reduce-scatter.20.cloned.1.call-start = ((), (), s32[]{:S(2)}) async-start(), calls=%async_computation.24 | async-start | bytes 2359296 | tf_op jit(solution)/shard_map/reduce_scatter | solution.py:748
  309.9 22.0 %all-to-all-start.3 = ((bf16[8,160,256]{2,1,0:T(8,128)(2,1)}), bf16[8,160,256]{2,1,0:T(8,128)(2,1)S(1)}, u32[]{:S(2)}, u32[]{:S(2)}) async-start(bf16[8,160,256]{2,1,0:T(8,128)(2,1)} %bitcast.175), calls=%async_computation.5 | async-start | bytes 1310720 | tf_op jit(solution)/shard_map/all_to_all | solution.py:685
  314.7 63.6 %reduce-scatter.18.cloned.1.call-start = ((), (), s32[]{:S(2)}) async-start(), calls=%async_computation.23 | async-start | bytes 4718592 | tf_op jit(solution)/shard_map/reduce_scatter | solution.py:741
  320.4 85.8 %reduce-scatter.14.cloned.1.call-start = ((), (), s32[]{:S(2)}) async-start(), calls=%async_computation.20 | async-start | bytes 1310720 | tf_op jit(solution)/shard_map/reduce_scatter | solution.py:733
  358.5 146.3 %all-reduce.7.cloned.1.call-start = ((), (), s32[]{:S(2)}) async-start(), calls=%async_computation.30 | async-start | bytes 4718592 | tf_op jit(solution)/shard_map/psum | solution.py:741
  378.3 207.4 %reduce-scatter.12.cloned.1.call-start = ((), (), s32[]{:S(2)}) async-start(), calls=%async_computation.19 | async-start | bytes 2949120 | tf_op jit(solution)/shard_map/reduce_scatter | solution.py:710
  382.9 249.5 %reduce-scatter.16.cloned.1.call-start = ((), (), s32[]{:S(2)}) async-start(), calls=%async_computation.21 | async-start | bytes 5242880 | tf_op jit(solution)/shard_map/reduce_scatter | solution.py:739
  386.3 297.5 %all-gather.32.cloned.1.call-start = ((), (), s32[]{:S(2)}) async-start(), calls=%async_computation.28 | async-start | bytes 2359296 | tf_op jit(solution)/shard_map/all_gather | solution.py:734
  406.2 304.7 %all-gather.26.cloned.1.call-start = ((), (), s32[]{:S(2)}) async-start(), calls=%async_computation.25 | async-start | bytes 2359296 | tf_op jit(solution)/shard_map/all_gather | solution.py:749
  504.8 252.5 %all-gather.34.cloned.1.call-start = ((), (), s32[]{:S(2)}) async-start(), calls=%async_computation.29 | async-start | bytes 4718592 | tf_op jit(solution)/shard_map/all_gather | solution.py:745
  514.4 25.1 %all-to-all-start.2 = ((bf16[8,20,1024]{2,1,0:T(8,128)(2,1)}), bf16[8,20,1024]{2,1,0:T(8,128)(2,1)S(1)}, u32[]{:S(2)}, u32[]{:S(2)}) async-start(bf16[8,20,1024]{2,1,0:T(8,128)(2,1)} %reshape.280), calls=%async_computation.4 | async-start | bytes 786432 | tf_op jit(solution)/shard_map/all_to_all | solution.py:713
  518.1 320.8 %all-reduce.5.cloned.1.call-start = ((), (), s32[]{:S(2)}) async-start(), calls=%async_computation.22 | async-start | bytes 2097152 | tf_op jit(solution)/shard_map/psum | solution.py:738
  (63 other events, 641.4 us)
Sparse Core Ops, SparseCore 0:
  10.2 57.3 all-gather.27
  69.8 15.2 all-gather.15
  86.7 34.4 all-gather.17
  122.6 44.9 all-gather.21
  169.5 18.1 all-gather.19
  189.7 27.1 all-gather.23
  218.5 18.1 all-gather.29
  247.4 26.5 reduce-scatter.9
  276.7 26.5 reduce-scatter.7
  305.9 26.0 reduce-scatter.19
  334.9 43.3 reduce-scatter.17
  381.3 24.8 reduce-scatter.13
  408.7 95.9 all-reduce.6
  509.1 76.5 reduce-scatter.11
  588.3 44.1 reduce-scatter.15
  634.4 49.2 all-gather.31
  685.2 25.6 all-gather.25
  712.3 44.9 all-gather.33
  760.8 78.0 all-reduce.4

commit v2 on v1

--- a/solution.py
+++ b/solution.py
@@ -3,6 +3,8 @@
 import jax
 import jax.numpy as jnp
 from jax import lax
+from jax.experimental import pallas as pl
+from jax.experimental.pallas import tpu as pltpu
 from jax.sharding import Mesh
 from jax.sharding import PartitionSpec as P
 
@@ -499,6 +501,7 @@
 
 CTX = ("z", "y")
 FSDP = ("x", "core")
+VMEM_BYTES = 56 << 20
 
 
 def norm_back(values, gain_vec, grad):
@@ -531,16 +534,519 @@
     return a.astype(jnp.bfloat16)
 
 
-def gather_ctx(block):
-    return lax.all_gather(block, CTX, axis=0, tiled=True)
-
-
-def gather_fsdp(block):
+def gather_fsdp_plain(block):
     return lax.all_gather(block, FSDP, axis=0, tiled=True)
 
 
-def gather_quad(block):
-    return lax.all_gather(block, ("y", "core"), axis=0, tiled=True)
+def over(block, axis):
+    return lax.ppermute(block, axis, [(0, 1), (1, 0)])
+
+
+def half_sum(block, axis):
+    place = lax.axis_index(axis)
+    got = over(lax.dynamic_index_in_dim(block, 1 - place, 0, keepdims=False), axis)
+    own = lax.dynamic_index_in_dim(block, place, 0, keepdims=False)
+    return low(own.astype(jnp.float32) + got.astype(jnp.float32))
+
+
+MESH_ID = pl.DeviceIdType.MESH
+LINE = 4
+
+
+class Net:
+    def __init__(self, send, recv):
+        self.send, self.recv, self.used = send, recv, 0
+        self.z, self.y, self.x, self.core = (lax.axis_index(a) for a in CTX + FSDP)
+        self.me = 2 * self.z + self.y
+        self.open = []
+
+    def at(self, dz=0, dy=0, dx=0, dc=0):
+        return (
+            self.z + dz,
+            1 - self.y if dy else self.y,
+            1 - self.x if dx else self.x,
+            1 - self.core if dc else self.core,
+        )
+
+    def put(self, src, dst, target, sends=None, recvs=None):
+        copy = Copy(self, src, dst, target, sends, recvs)
+        self.open.append(copy)
+        return copy
+
+    def close(self):
+        for copy in self.open:
+            copy.arrived()
+        for copy in self.open:
+            copy.left()
+
+
+def guarded(condition, action):
+    if condition is None:
+        action()
+    else:
+        pl.when(condition)(action)
+
+
+class Copy:
+    def __init__(self, net, src, dst, target, sends, recvs):
+        i = net.used
+        net.used += 1
+        self.sends, self.recvs, self.waited = sends, recvs, False
+        self.copy = pltpu.make_async_remote_copy(
+            src, dst, net.send.at[i], net.recv.at[i], device_id=target, device_id_type=MESH_ID
+        )
+        guarded(sends, self.copy.start)
+
+    def arrived(self):
+        if not self.waited:
+            self.waited = True
+            guarded(self.recvs, self.copy.wait_recv)
+
+    def left(self):
+        guarded(self.sends, self.copy.wait_send)
+
+
+def greet(net, kinds):
+    barrier = pltpu.get_barrier_semaphore()
+    partners = []
+    if "z" in kinds:
+        partners += [(net.at(dz=1), net.z < LINE - 1), (net.at(dz=-1), net.z > 0)]
+    if "y" in kinds:
+        partners.append((net.at(dy=1), None))
+    if "x" in kinds:
+        partners.append((net.at(dx=1), None))
+    if "core" in kinds:
+        partners.append((net.at(dc=1), None))
+    if "ctx" in kinds:
+        for k in range(1, 2 * LINE):
+            other = lax.rem(net.me + k, 2 * LINE)
+            partners.append(((other // 2, lax.rem(other, 2), net.x, net.core), None))
+    for target, there in partners:
+        guarded(
+            there,
+            lambda target=target: pl.semaphore_signal(
+                barrier, inc=1, device_id=target, device_id_type=MESH_ID
+            ),
+        )
+    ends = 0
+    if "z" in kinds:
+        ends = (net.z == 0).astype(jnp.int32) + (net.z == LINE - 1).astype(jnp.int32)
+    pl.semaphore_wait(barrier, len(partners) - ends)
+
+
+def drive(*programs):
+    live = list(programs)
+    while live:
+        for program in list(live):
+            if next(program, "end") == "end":
+                live.remove(program)
+
+
+def along_line(net, own, view, sides, slot):
+    z = net.z
+    up = net.put(own, view(slot(z)), net.at(dz=1), z < LINE - 1, z > 0)
+    down = net.put(own, view(slot(z)), net.at(dz=-1), z > 0, z < LINE - 1)
+    for s in range(1, LINE):
+        from_low, from_high = z >= s, z + s <= LINE - 1
+        up.arrived()
+        low_block, high_block = view(slot(z - s)), view(slot(z + s))
+        if s < LINE - 1:
+            up = net.put(low_block, low_block, net.at(dz=1), from_low & (z < LINE - 1), z >= s + 1)
+        if sides:
+            net.put(low_block, low_block, net.at(dy=1), from_low, from_low)
+        down.arrived()
+        if s < LINE - 1:
+            down = net.put(
+                high_block, high_block, net.at(dz=-1), from_high & (z > 0), z + s + 1 <= LINE - 1
+            )
+        if sides:
+            net.put(high_block, high_block, net.at(dy=1), from_high, from_high)
+        yield
+
+
+def gather_line_first(net, own, view):
+    net.put(own, view(net.me), net.at(dy=1))
+    yield from along_line(net, own, view, True, lambda z: 2 * z + net.y)
+
+
+def gather_side_first(net, own, view):
+    side = net.put(own, view(net.me), net.at(dy=1))
+    first = along_line(net, own, view, False, lambda z: 2 * z + net.y)
+    yield next(first)
+    side.arrived()
+    other = view(net.me + 1 - 2 * net.y)
+    second = along_line(net, other, view, False, lambda z: 2 * z + 1 - net.y)
+    for _ in second:
+        next(first, None)
+        yield
+
+
+def gather_ctx_programs(net, own, out, cut):
+    rows = own.shape[0]
+    programs = [
+        gather_line_first(
+            net, own.at[pl.ds(0, cut)], lambda slot: out.at[slot, pl.ds(0, cut)]
+        )
+    ]
+    if cut < rows:
+        rest = pl.ds(cut, rows - cut)
+        programs.append(gather_side_first(net, own.at[rest], lambda slot: out.at[slot, rest]))
+    return programs
+
+
+def gather_fsdp(net, own, out):
+    f = 2 * net.x + net.core
+    net.put(own, out.at[f], net.at(dc=1))
+    over = net.put(own, out.at[f], net.at(dx=1))
+    yield
+    yield
+    yield
+    over.arrived()
+    far = out.at[2 * (1 - net.x) + net.core]
+    net.put(far, far, net.at(dc=1))
+    yield
+
+
+def gather_quad(net, own, out):
+    q = 2 * net.y + net.core
+    net.put(own, out.at[q], net.at(dc=1))
+    over = net.put(own, out.at[q], net.at(dy=1))
+    yield
+    over.arrived()
+    far = out.at[2 * (1 - net.y) + net.core]
+    net.put(far, far, net.at(dc=1))
+    yield
+
+
+def swap_ctx(net, blocks, out):
+    for k in range(1, 2 * LINE):
+        other = lax.rem(net.me + k, 2 * LINE)
+        net.put(
+            blocks.at[other], out.at[net.me], (other // 2, lax.rem(other, 2), net.x, net.core)
+        )
+    yield
+
+
+def own_copies(pairs, sem):
+    copies = [pltpu.make_async_copy(src, dst, sem.at[i]) for i, (src, dst) in enumerate(pairs)]
+    for copy in copies:
+        copy.start()
+    return copies
+
+
+def net_call(body, outs, args, copies, locals_, number, scratch=(), vmem=()):
+    def kernel(*refs):
+        *rest, send, recv, local = refs
+        net = Net(send, recv)
+        body(net, local, *rest)
+        assert net.used <= copies, net.used
+
+    any_space = pl.BlockSpec(memory_space=pl.ANY)
+    in_vmem = pl.BlockSpec(memory_space=pltpu.VMEM)
+    count = len(args)
+    return pl.pallas_call(
+        kernel,
+        out_shape=outs,
+        in_specs=[in_vmem if i in vmem else any_space for i in range(count)],
+        out_specs=[in_vmem if count + i in vmem else any_space for i in range(len(outs))],
+        scratch_shapes=list(scratch)
+        + [
+            pltpu.SemaphoreType.DMA((copies,)),
+            pltpu.SemaphoreType.DMA((copies,)),
+            pltpu.SemaphoreType.DMA((max(1, locals_),)),
+        ],
+        compiler_params=pltpu.CompilerParams(
+            collective_id=number, has_side_effects=True, vmem_limit_bytes=VMEM_BYTES
+        ),
+    )(*args)
+
+
+def shape_of(*dims, kind=jnp.bfloat16):
+    return jax.ShapeDtypeStruct(dims, kind)
+
+
+def gather_first(tokens, w_qkv, gains):
+    rows = tokens.shape[0]
+
+    def body(net, local, tok, wts, gns, tok_all, wts_all, gns_all):
+        greet(net, ("z", "y", "x", "core"))
+        f = 2 * net.x + net.core
+        mine = own_copies(
+            [(tok, tok_all.at[net.me]), (wts, wts_all.at[f]), (gns, gns_all.at[f])], local
+        )
+        drive(
+            *gather_ctx_programs(net, tok, tok_all, rows * 4 // 5),
+            gather_fsdp(net, wts, wts_all),
+            gather_fsdp(net, gns, gns_all),
+        )
+        for copy in mine:
+            copy.wait()
+        net.close()
+
+    return net_call(
+        body,
+        [
+            shape_of(2 * LINE, *tokens.shape),
+            shape_of(4, *w_qkv.shape),
+            shape_of(4, *gains.shape),
+        ],
+        [tokens, w_qkv, gains],
+        40,
+        3,
+        0,
+    )
+
+
+def swap_heads(blocks, number):
+    def body(net, local, src, out):
+        greet(net, ("ctx",))
+        mine = own_copies([(src.at[net.me], out.at[net.me])], local)
+        drive(swap_ctx(net, src, out))
+        mine[0].wait()
+        net.close()
+
+    return net_call(body, [shape_of(*blocks.shape)], [blocks], 8, 1, number)[0]
+
+
+def swap_two(first, second, number):
+    def body(net, local, a, b, a_out, b_out):
+        greet(net, ("ctx",))
+        mine = own_copies(
+            [(a.at[net.me], a_out.at[net.me]), (b.at[net.me], b_out.at[net.me])], local
+        )
+        drive(swap_ctx(net, a, a_out), swap_ctx(net, b, b_out))
+        for copy in mine:
+            copy.wait()
+        net.close()
+
+    return net_call(
+        body, [shape_of(*first.shape), shape_of(*second.shape)], [first, second], 16, 2, number
+    )
+
+
+def gather_four(block, number):
+    def body(net, local, own, out):
+        greet(net, ("y", "core"))
+        mine = own_copies([(own, out.at[2 * net.y + net.core])], local)
+        drive(gather_quad(net, own, out))
+        mine[0].wait()
+        net.close()
+
+    return net_call(body, [shape_of(4, *block.shape)], [block], 8, 1, number)[0]
+
+
+def scatter_four(parts, number):
+    _, rows, cols = parts.shape
+
+    def body(net, local, src, out, from_core, near, from_side):
+        greet(net, ("y", "core"))
+        own, beside = 2 * net.y + net.core, 2 * net.y + 1 - net.core
+        far, far_beside = 2 * (1 - net.y) + net.core, 2 * (1 - net.y) + 1 - net.core
+        one = net.put(src.at[far_beside], from_core.at[0], net.at(dc=1))
+        two = net.put(src.at[beside], from_core.at[1], net.at(dc=1))
+        one.arrived()
+        near[...] = low(src[far].astype(jnp.float32) + from_core[0].astype(jnp.float32))
+        side = net.put(near, from_side, net.at(dy=1))
+        two.arrived()
+        out[...] = src[own].astype(jnp.float32) + from_core[1].astype(jnp.float32)
+        side.arrived()
+        out[...] += from_side[...].astype(jnp.float32)
+        net.close()
+
+    block = (rows, cols)
+    return net_call(
+        body,
+        [shape_of(*block, kind=jnp.float32)],
+        [parts],
+        4,
+        0,
+        number,
+        scratch=[
+            pltpu.VMEM((2, *block), jnp.bfloat16),
+            pltpu.VMEM(block, jnp.bfloat16),
+            pltpu.VMEM(block, jnp.bfloat16),
+        ],
+        vmem=(0, 1),
+    )[0]
+
+
+def sum_line(net, held, send_up, send_down, got_up, got_down, ready):
+    z = net.z
+    ups, downs = [], []
+
+    def fill(send, got, block, t, first):
+        def alone():
+            send[t] = low(held[block])
+
+        def added():
+            send[t] = low(held[block] + got[t - 1].astype(jnp.float32))
+
+        return alone if first else added
+
+    for t in range(LINE - 1):
+        ready(t)
+        to_up, to_down = LINE - 1 - t + z, z - LINE + 1 + t
+        up_on, down_on = (z <= t) & (z < LINE - 1), (z >= LINE - 1 - t) & (z > 0)
+        pl.when(z == 0)(fill(send_up, got_up, to_up, t, True))
+        pl.when(z == LINE - 1)(fill(send_down, got_down, to_down, t, True))
+        if t:
+            pl.when(up_on & (z >= 1))(fill(send_up, got_up, to_up, t, False))
+            pl.when(down_on & (z <= LINE - 2))(fill(send_down, got_down, to_down, t, False))
+        ups.append(
+            net.put(
+                send_up.at[t], got_up.at[t], net.at(dz=1), up_on, (z >= 1) & (z - 1 <= t)
+            )
+        )
+        downs.append(
+            net.put(
+                send_down.at[t],
+                got_down.at[t],
+                net.at(dz=-1),
+                down_on,
+                (z <= LINE - 2) & (z + 1 >= LINE - 1 - t),
+            )
+        )
+        yield
+        ups[t].arrived()
+        downs[t].arrived()
+    ready(LINE - 1)
+    last = LINE - 2
+
+    def add_up():
+        held[z] += got_up[last].astype(jnp.float32)
+
+    def add_down():
+        held[z] += got_down[last].astype(jnp.float32)
+
+    pl.when(z >= 1)(add_up)
+    pl.when(z <= LINE - 2)(add_down)
+    yield
+
+
+def far_first(z):
+    return [
+        jnp.where(z < 2, 3, 0),
+        jnp.where(z < 2, 2, 1),
+        z + 1 - 2 * lax.rem(z, 2),
+        z,
+    ]
+
+
+def line_scratch(rows, cols):
+    line = pltpu.VMEM((LINE - 1, rows, cols), jnp.bfloat16)
+    return [pltpu.VMEM((LINE, rows, cols), jnp.float32), line, line, line, line]
+
+
+def sum_sides(net, src, from_side, line):
+    z, y = net.z, net.y
+    held = line[0]
+    order = far_first(z)
+    sides = [net.put(src.at[2 * k + 1 - y], from_side.at[k], net.at(dy=1)) for k in order]
+
+    def ready(t):
+        k = order[t]
+        sides[t].arrived()
+        held[k] = src[2 * k + y].astype(jnp.float32) + from_side[k].astype(jnp.float32)
+
+    yield from sum_line(net, *line, ready)
+
+
+def scatter_ctx(parts, number):
+    _, rows, cols = parts.shape
+
+    def body(net, local, src, out, from_side, *line):
+        greet(net, ("z", "y"))
+        drive(sum_sides(net, src, from_side, line))
+        out[...] = line[0][net.z]
+        net.close()
+
+    return net_call(
+        body,
+        [shape_of(rows, cols, kind=jnp.float32)],
+        [parts],
+        12,
+        0,
+        number,
+        scratch=[pltpu.VMEM((LINE, rows, cols), jnp.bfloat16)] + line_scratch(rows, cols),
+        vmem=(0, 1),
+    )[0]
+
+
+def sum_and_gather(gate_up, down, out_proj, heads, number):
+    _, _, gu_rows, gu_cols = gate_up.shape
+    dn_rows, dn_cols = down.shape[1:]
+    o_rows, o_cols = out_proj.shape[1:]
+
+    def body(net, local, gu, dn, op, hd, gu_all, dn_all, op_all, hd_all, *scratch):
+        gu_line, dn_line, op_line = scratch[:5], scratch[5:10], scratch[10:15]
+        op_side, gu_low, gu_pair, dn_low, op_low = scratch[15:]
+        greet(net, ("z", "y", "core"))
+        z, core = net.z, net.core
+        mine = own_copies([(hd, hd_all.at[net.me])], local)
+
+        def gu_ready(t):
+            k = far_first(z)[t]
+            for c in range(2):
+                gu_line[0][k, pl.ds(c * gu_rows, gu_rows)] = gu[k, c].astype(jnp.float32)
+
+        def dn_ready(t):
+            k = far_first(z)[t]
+            dn_line[0][k] = dn[k].astype(jnp.float32)
+
+        drive(
+            sum_line(net, *gu_line, gu_ready),
+            sum_line(net, *dn_line, dn_ready),
+            sum_sides(net, op, op_side, op_line),
+        )
+        dn_low[...] = low(dn_line[0][z])
+        op_low[...] = low(op_line[0][z])
+        for c in range(2):
+            gu_low[c] = low(gu_line[0][z, pl.ds(c * gu_rows, gu_rows)])
+        swap = net.put(gu_low.at[1 - core], gu_pair.at[core], net.at(dc=1))
+        gu_pair[core] = gu_low[core]
+        swap.arrived()
+        rest = own_copies(
+            [
+                (gu_pair, gu_all.at[net.me]),
+                (dn_low, dn_all.at[net.me]),
+                (op_low, op_all.at[net.me]),
+            ],
+            local.at[pl.ds(1, 3)],
+        )
+        drive(
+            gather_line_first(net, gu_pair, lambda slot: gu_all.at[slot]),
+            gather_line_first(net, dn_low, lambda slot: dn_all.at[slot]),
+            gather_line_first(net, op_low, lambda slot: op_all.at[slot]),
+            gather_side_first(net, hd, lambda slot: hd_all.at[slot]),
+        )
+        for copy in mine + rest:
+            copy.wait()
+        net.close()
+
+    return net_call(
+        body,
+        [
+            shape_of(2 * LINE, 2, gu_rows, gu_cols),
+            shape_of(2 * LINE, dn_rows, dn_cols),
+            shape_of(2 * LINE, o_rows, o_cols),
+            shape_of(2 * LINE, *heads.shape),
+        ],
+        [gate_up, down, out_proj, heads],
+        96,
+        4,
+        number,
+        scratch=line_scratch(2 * gu_rows, gu_cols)
+        + line_scratch(dn_rows, dn_cols)
+        + line_scratch(o_rows, o_cols)
+        + [
+            pltpu.VMEM((LINE, o_rows, o_cols), jnp.bfloat16),
+            pltpu.VMEM((2, gu_rows, gu_cols), jnp.bfloat16),
+            pltpu.VMEM((2, gu_rows, gu_cols), jnp.bfloat16),
+            pltpu.VMEM((dn_rows, dn_cols), jnp.bfloat16),
+            pltpu.VMEM((o_rows, o_cols), jnp.bfloat16),
+        ],
+        vmem=(0, 1, 2),
+    )
 
 
 def fast_layer(
@@ -588,11 +1094,6 @@
     to_dealt = low(dealt_index[:, None] == ids[None, :])
 
     packed_gain = jnp.concatenate([attn_gain, mlp_gain, query_norm_gain, k_gain])[None]
-    gains = gather_fsdp(packed_gain).astype(jnp.float32)
-    a_gain = gains[:, :256].reshape(-1)
-    m_gain = gains[:, 256:512].reshape(-1)
-    q_gain = gains[:, 512:544].reshape(-1)
-    k_gain_all = gains[:, 544:576].reshape(-1)
     qkv_own = jnp.concatenate(
         [
             lax.dynamic_slice_in_dim(w_q, here * width, width, 1),
@@ -601,8 +1102,14 @@
         ],
         axis=1,
     )
-    all_tokens = gather_ctx(tokens[0])
-    w_qkv = gather_fsdp(qkv_own)
+    all_tokens, w_qkv, gains = gather_first(tokens[0], qkv_own, jnp.tile(packed_gain, (16, 1)))
+    all_tokens = all_tokens.reshape(count, MODEL_WIDTH)
+    w_qkv = w_qkv.reshape(MODEL_WIDTH, -1)
+    gains = gains[:, 0].astype(jnp.float32)
+    a_gain = gains[:, :256].reshape(-1)
+    m_gain = gains[:, 256:512].reshape(-1)
+    q_gain = gains[:, 512:544].reshape(-1)
+    k_gain_all = gains[:, 544:576].reshape(-1)
     values = all_tokens.astype(jnp.float32)
     normed = low(root_mean_norm(values, a_gain))
     qkv = dot(normed, w_qkv)
@@ -628,12 +1135,12 @@
     )
     mixed_heads = low(jnp.transpose(mixed, (1, 0, 2)).reshape(count, width))
     mixed_out = low(dot(to_dealt, mixed_heads)).reshape(slots, rows, width)
-    mixed_in = lax.all_to_all(mixed_out, CTX, 0, 0, tiled=True)
+    mixed_in = swap_heads(mixed_out, 1)
     mixed_low = jnp.transpose(mixed_in, (1, 0, 2)).reshape(rows, slots * width)
 
     own_rows = lax.dynamic_slice_in_dim(to_dealt, here * rows, rows, 0)
     residual = dot(own_rows, all_tokens)
-    full_o = gather_fsdp(w_o)
+    full_o = gather_fsdp_plain(w_o)
     middle = residual + dot(mixed_low, full_o)
     normed2 = low(root_mean_norm(middle, m_gain))
 
@@ -656,25 +1163,23 @@
     w_gu = lax.all_gather(sides, "x", axis=0, tiled=True).reshape(-1, 4 * ff_half)
     down_own = lax.dynamic_slice_in_dim(w_down, y * ff_half, ff_half, 0)
     w_dn = lax.all_gather(down_own, "x", axis=0, tiled=True)
-    quad_n = gather_quad(normed2)
-    quad_g = gather_quad(out_cotangent[0])
+    quad_n = gather_four(normed2, 2).reshape(4 * rows, -1)
+    quad_g = gather_four(out_cotangent[0], 3).reshape(4 * rows, -1)
     gate_up = dot(quad_n, w_gu)
     gate, up = gate_up[:, : 2 * ff_half], gate_up[:, 2 * ff_half :]
     sig = 1.0 / (1.0 + jnp.exp(-gate))
     silu = gate * sig
     hidden = low(silu * up)
     partial_out = low(dot(hidden, w_dn))
-    out_sum = lax.psum_scatter(partial_out, ("y", "core"), scatter_dimension=0, tiled=True)
-    output = low(middle + out_sum.astype(jnp.float32))
+    out_sum = scatter_four(partial_out.reshape(4, rows, -1), 4)
+    output = low(middle + out_sum)
 
     d_hidden = dot_trans(quad_g, w_dn)
     d_gate = low(d_hidden * up * (sig * (1.0 + gate * (1.0 - sig))))
     d_up = low(d_hidden * silu)
     d_gu = jnp.concatenate([d_gate, d_up], axis=1)
     dn2_part = low(dot_trans(d_gu, w_gu))
-    d_normed2 = lax.psum_scatter(
-        dn2_part, ("y", "core"), scatter_dimension=0, tiled=True
-    ).astype(jnp.float32)
+    d_normed2 = scatter_four(dn2_part.reshape(4, rows, -1), 5)
     grad_gu = low(outer_rows(quad_n, d_gu))
     grad_dn = low(outer_rows(hidden, quad_g))
     dx2, dg2 = norm_back(middle, m_gain, d_normed2)
@@ -682,7 +1187,11 @@
     middle_low = low(d_middle)
     d_mixed_tok = low(dot_trans(middle_low, full_o))
     dm_out = jnp.transpose(d_mixed_tok.reshape(rows, slots, width), (1, 0, 2))
-    dm_in = lax.all_to_all(dm_out, CTX, 0, 0, tiled=True).reshape(count, width)
+    padded = jnp.pad(
+        middle_low.reshape(slots, piece, MODEL_WIDTH), ((0, 0), (0, 32 - piece), (0, 0))
+    )
+    dm_in, back = swap_two(dm_out, padded, 6)
+    dm_in = dm_in.reshape(count, width)
     d_mixed = low(
         lax.dot_general(
             to_dealt, dm_in, (((0,), (0,)), ((), ())), preferred_element_type=jnp.float32
@@ -707,12 +1216,11 @@
     d_k_pre, dg_k = norm_back(k_pre, k_gain_all, rope_back(d_k, cosine, sine))
     d_qkv = jnp.concatenate([low(d_q_pre.reshape(count, width)), low(d_k_pre), low(d_v)], axis=1)
     dn_part = low(dot_trans(d_qkv, w_qkv))
-    d_normed = lax.psum_scatter(dn_part, CTX, scatter_dimension=0, tiled=True).astype(jnp.float32)
+    d_normed = scatter_ctx(dn_part.reshape(slots, rows, -1), 7)
     grad_qkv = low(outer_rows(normed, d_qkv))
 
-    back = lax.all_to_all(middle_low.reshape(slots, piece, MODEL_WIDTH), CTX, 0, 0, tiled=True)
     own_plan = lax.dynamic_index_in_dim(plan, here, 0, keepdims=False)
-    d_middle_given = jnp.take(back, own_plan, axis=0).reshape(rows, MODEL_WIDTH)
+    d_middle_given = jnp.take(back[:, :piece], own_plan, axis=0).reshape(rows, MODEL_WIDTH)
     dx1, dg1 = norm_back(tokens[0].astype(jnp.float32), a_gain, d_normed)
     input_grad = d_middle_given.astype(jnp.float32) + dx1
 
@@ -730,23 +1238,25 @@
     )
     own_gain = lax.dynamic_index_in_dim(gain_sums, 2 * x + core, 0, keepdims=False)
 
-    qkv_sum = lax.psum_scatter(grad_qkv, FSDP, scatter_dimension=0, tiled=True)
-    qkv_all = lax.all_gather(qkv_sum, CTX, axis=0)
+    def halves(a):
+        return a.reshape(2, a.shape[0] // 2, *a.shape[1:])
+
+    def by_core(a):
+        return jnp.swapaxes(a.reshape(2, 2, -1, a.shape[-1]), 0, 1)
+
+    gu_half = half_sum(halves(grad_gu), "x")
+    gu_blocks = jnp.swapaxes(gu_half.reshape(2, LINE, -1, 4 * ff_half), 0, 1)
+    dn_half = half_sum(halves(grad_dn), "x").reshape(LINE, -1, MODEL_WIDTH)
+    o_half = half_sum(half_sum(by_core(grad_o), "core"), "x").reshape(slots, -1, MODEL_WIDTH)
+    qkv_sum = half_sum(half_sum(by_core(grad_qkv), "core"), "x")
+    gu_all, dn_all, o_all, qkv_all = sum_and_gather(gu_blocks, dn_half, o_half, qkv_sum, 8)
     q_all = jnp.transpose(qkv_all[:, :, :width], (1, 0, 2)).reshape(-1, slots * width)
     k_all = jnp.transpose(qkv_all[:, :, width : width + HEAD_SIZE], (1, 0, 2))
     v_all = jnp.transpose(qkv_all[:, :, width + HEAD_SIZE :], (1, 0, 2))
-    o_sum = lax.psum(
-        lax.psum_scatter(grad_o, FSDP, scatter_dimension=0, tiled=True), CTX
-    )
-    gu_sum = lax.psum(lax.psum_scatter(grad_gu, "x", scatter_dimension=0, tiled=True), "z")
-    gu_pair = lax.all_to_all(
-        gu_sum.reshape(2, -1, 4 * ff_half), "core", 0, 0, tiled=True
-    )
-    gu_all = lax.all_gather(gu_pair, "y", axis=0)
-    gu_all = gu_all.reshape(2, 2, -1, 2, 2, ff_half)
-    gu_all = jnp.transpose(gu_all, (3, 2, 4, 1, 0, 5)).reshape(2, -1, 8 * ff_half)
-    dn_sum = lax.psum(lax.psum_scatter(grad_dn, "x", scatter_dimension=0, tiled=True), "z")
-    dn_all = lax.all_gather(dn_sum, "y", axis=0, tiled=True)
+    o_sum = o_all.reshape(-1, MODEL_WIDTH)
+    gu_all = gu_all.reshape(LINE, 2, 2, -1, 2, 2, ff_half)
+    gu_all = jnp.transpose(gu_all, (4, 0, 3, 5, 2, 1, 6)).reshape(2, -1, 8 * ff_half)
+    dn_all = jnp.swapaxes(dn_all.reshape(LINE, 2, -1, MODEL_WIDTH), 0, 1).reshape(-1, MODEL_WIDTH)
 
     def wide(a):
         return a.astype(jnp.float32)

time: 859 us -> 596 us (0.69)
  waiting for transfers between devices: 588 us -> 19.2 us
  Pallas kernels: 0 us -> 316 us
  blocking collectives: 62.4 us -> 50.2 us
  starting transfers between devices: 15 us -> 5.09 us
    pallas_call x0 -> x9, Pallas kernels: none -> 316 us  [net_call(): pl.pallas_call(kernel, out_shape=outs, in_specs=[in_vmem if i in vmem els...]
    all_gather x8 -> x1, waiting for transfers between devices: 202 us -> 0.01 us  [gather_fsdp_plain(): return lax.all_gather(block, FSDP, axis=0, tiled=True)]
    psum x2 -> x0, waiting for transfers between devices: 151 us -> none  [the longest x1 98.5 us: fast_layer(): lax.psum(lax.psum_scatter(grad_gu, 'x', scatter_dimension=0, tiled=True),...]
    reduce_scatter x7 -> x0, waiting for transfers between devices: 135 us -> none  [the longest x1 45.3 us: fast_layer(): lax.psum_scatter(dn_part, CTX, scatter_dimension=0, tiled=True)]
    all_to_all x3 -> x0, waiting for transfers between devices: 47.3 us -> none  [the longest x1 20.6 us: fast_layer(): lax.all_to_all(middle_low.reshape(slots, piece, MODEL_WIDTH), CTX, 0, 0,...]
    all_gather x1, waiting for transfers between devices: 27.3 us -> 0.02 us  [fast_layer(): lax.all_gather(sides, 'x', axis=0, tiled=True).reshape(-1, 4 * ff_half)]
    all_gather x1, waiting for transfers between devices: 22.8 us -> 0.01 us  [fast_layer(): w_dn = lax.all_gather(down_own, 'x', axis=0, tiled=True)]
    ppermute x0 -> x6, waiting for transfers between devices: none -> 18.5 us  [over(): return lax.ppermute(block, axis, [(0, 1), (1, 0)])]
  transfers between devices with their start and end apart: 22 -> 9, of which waited for: 20 -> 2; matrix products, arithmetic and copies ran while one was open for 17% -> 12% of each run, Pallas kernels for 0% -> 20%
where the time goes in v2:
time: 596 us; the launch traced here: 586 us
  Pallas kernels  316 us (53%)
  matrix products  72.7 us (12%)
  local copies, waits for them, and re-layouts  60.8 us (10%)
  blocking collectives  50.2 us (8%)
  other arithmetic  46.2 us (8%)
  waiting for transfers between devices  19.2 us (3%)
  between operations  15.2 us (3%)
    pallas_call x9, Pallas kernels, net_call(): pl.pallas_call(kernel, out_shape=outs, in_specs=[in_vmem if i in vmem els...  316 us
    psum x1, blocking collectives, fast_layer(): lax.psum(jnp.concatenate([jnp.sum(dg1, axis=0).reshape(4, 256), jnp.sum(d...  44.3 us
    convert_element_type x8, local copies, waits for them, and re-layouts, wide(): return a.astype(jnp.float32)  18.5 us
    ppermute x6, waiting for transfers between devices, over(): return lax.ppermute(block, axis, [(0, 1), (1, 0)])  18.5 us
    dot_general x6, matrix products, dot(): return jnp.dot(a, b, preferred_element_type=jnp.float32)  17.2 us
    dot_general x4, matrix products, dot_trans(): lax.dot_general(left_side, right_side, (((1,), (1,)), ((), ())), preferre...  15.6 us
    convert_element_type x12, other arithmetic, low(): return a.astype(jnp.bfloat16)  14.5 us
    unnamed x121, local copies, waits for them, and re-layouts  14 us
  transfers between devices with their start and end apart: 9, of which 2 were waited for; matrix products, arithmetic and copies ran while one was open for 12% of the time, Pallas kernels for 20%

profile of v2, /device:TPU:0, one launch (start us, length us, event | category | flops | bytes accessed | tf_op | source)
XLA Modules:
  0.0 585.6 jit_solution(4174247899436699417)
XLA Ops:
  9.9 5.9 %all_to_all.5 = bf16[2,256,1536]{2,1,0:T(8,128)(2,1)} all-to-all(bf16[2,256,1536]{2,1,0:T(8,128)(2,1)S(1)} %pad_maximum_fusion.1), channel_id=1, replica_groups=mesh['z'=4,'y'=2,'x'=2,'core'=2] {'core'}, dimensions={0} | all-to-all | bytes 3145728 | tf_op jit(solution)/shard_map/all_to_all | solution.py:1162
  20.2 39.8 %shard_map.246 = (bf16[8,160,1024]{2,1,0:T(8,128)(2,1)}, bf16[4,256,512]{2,1,0:T(8,128)(2,1)}, bf16[4,16,576]{2,1,0:T(8,128)(2,1)}) custom-call(bf16[160,1024]{1,0:T(8,128)(2,1)} %bitcast.225, bf16[256,512]{1,0:T(8,128)(2,1)} %pad_maximum_fusion.9.refs_1_, bf16[16,576]{1,0:T(8,128)(2,1)} %tile.2.refs_2_), custom_call_target="tpu_custom_call" | custom-call | tf_op jit(solution)/shard_map/pallas_call | solution.py:747
  83.1 3.7 fusion.43
  91.7 14.7 %shard_map.247 = bf16[8,160,256]{2,1,0:T(8,128)(2,1)} custom-call(bf16[8,160,256]{2,1,0:T(8,128)(2,1)} %bitcast.254), custom_call_target="tpu_custom_call" | custom-call | tf_op jit(solution)/shard_map/pallas_call | solution.py:747
  107.6 13.5 %shard_map.250 = bf16[4,160,1024]{2,1,0:T(8,128)(2,1)} custom-call(bf16[160,1024]{1,0:T(8,128)(2,1)} %bitcast.245), custom_call_target="tpu_custom_call" | custom-call | tf_op jit(solution)/shard_map/pallas_call | solution.py:747
  127.1 11.3 %shard_map.248 = bf16[4,160,1024]{2,1,0:T(8,128)(2,1)} custom-call(bf16[160,1024]{1,0:T(8,128)(2,1)} %multiply_convert_fusion.5.refs_0_), custom_call_target="tpu_custom_call" | custom-call | tf_op jit(solution)/shard_map/pallas_call | solution.py:747
  138.4 6.4 %fusion.75 = f32[640,1536]{1,0:T(8,128)} fusion(bf16[640,1024]{1,0:T(8,128)(2,1)} %bitcast.243, bf16[1024,1536]{1,0:T(8,128)(2,1)} %bitcast.270), kind=kOutput, calls=%fused_computation.209 | convolution fusion | flops 2013265920 | bytes 8388608 | tf_op jit(solution)/shard_map/dot_general | solution.py:530
  144.9 6.2 %fusion.35 = (bf16[640,768]{1,0:T(8,128)(2,1)}, bf16[640,768]{1,0:T(8,128)(2,1)}, bf16[640,768]{1,0:T(8,128)(2,1)S(1)}) fusion(f32[640,1536]{1,0:T(8,128)} %fusion.75, bf16[768,1024]{1,0:T(8,128)(2,1)} %all-gather.8.cloned.1.call-done, bf16[640,1024]{1,0:T(8,128)(2,1)} %bitcast.241), kind=kOutput, calls=%fused_computation.57 | convolution fusion | flops 1014005760 | bytes 9764864 | tf_op jit(solution)/shard_map/dot_general | solution.py:39
  153.3 13.9 %shard_map.249 = f32[160,1024]{1,0:T(8,128)} custom-call(bf16[4,160,1024]{2,1,0:T(8,128)(2,1)} %bitcast.246), custom_call_target="tpu_custom_call" | custom-call | tf_op jit(solution)/shard_map/pallas_call | solution.py:747
  167.3 4.8 convolution_convert_fusion.6
  172.0 13.4 %shard_map.251 = f32[160,1024]{1,0:T(8,128)} custom-call(bf16[4,160,1024]{2,1,0:T(8,128)(2,1)} %bitcast.247), custom_call_target="tpu_custom_call" | custom-call | tf_op jit(solution)/shard_map/pallas_call | solution.py:747
  190.0 4.6 convolution_convert_fusion.1
  197.2 4.5 convolution_convert_fusion
  205.0 29.4 %shard_map.252 = (bf16[8,160,256]{2,1,0:T(8,128)(2,1)}, bf16[8,32,1024]{2,1,0:T(8,128)(2,1)}) custom-call(bf16[8,160,256]{2,1,0:T(8,128)(2,1)} %bitcast.235, bf16[8,32,1024]{2,1,0:T(8,128)(2,1)} %pad.4.refs_1_), custom_call_target="tpu_custom_call" | custom-call | tf_op jit(solution)/shard_map/pallas_call | solution.py:747
  237.5 6.5 %fusion.30 = bf16[1280,128]{0,1:T(8,128)(2,1)S(1)} fusion(bf16[1280,2,128]{0,2,1:T(8,128)(2,1)S(1)} %bitcast.252, f32[2,1280,1280]{1,2,0:T(8,128)} %copy-done.4, f32[2,1280]{1,0:T(2,128)S(1)} %log_add_fusion, pred[1280,1280]{0,1:T(8,128)(4,1)S(1)} %copy-done.35), kind=kOutput, calls=%fused_computation.48 | convolution fusion | flops 848855040 | bytes 15738880 | tf_op jit(solution)/shard_map/gtu,tgh->uh/dot_general | solution.py:1208
  244.0 7.1 %fusion.1 = bf16[2,1280,1280]{1,2,0:T(8,128)(2,1)S(1)} fusion(bf16[1280,2,128]{0,2,1:T(8,128)(2,1)S(1)} %bitcast.253, f32[2,1280,1280]{1,2,0:T(8,128)} %copy-done.4, f32[2,1280]{1,0:T(2,128)S(1)} %fusion.42, f32[2,1280]{1,0:T(2,128)S(1)} %log_add_fusion, pred[1280,1280]{0,1:T(8,128)(4,1)S(1)} %copy-done.35, f32[1280,512]{0,1:T(8,128)S(1)} %fusion.73), kind=kOutput, calls=%fused_computation.4 | convolution fusion | flops 855244800 | bytes 22302720 | tf_op jit(solution)/shard_map/tgh,uh->gtu/dot_general | solution.py:1206
  271.2 37.5 %shard_map.253 = f32[160,1024]{1,0:T(8,128)} custom-call(bf16[8,160,1024]{2,1,0:T(8,128)(2,1)} %bitcast.234), custom_call_target="tpu_custom_call" | custom-call | tf_op jit(solution)/shard_map/pallas_call | solution.py:747
  310.4 44.3 %psum.7 = f32[4,576]{1,0:T(4,128)S(1)} all-reduce(f32[4,576]{1,0:T(4,128)S(1)} %pad_maximum_fusion.10), channel_id=1, replica_groups=mesh['z'=4,'y'=2,'x'=2,'core'=2] {'z','y','x','core'}, use_global_device_ids=true, to_apply=%region_19.20 | all-reduce | flops 2304 | bytes 18432 | tf_op jit(solution)/shard_map/psum | solution.py:1227
  366.9 4.4 collective-permute-done.5
  377.5 14.0 %collective-permute-done.3 = bf16[512,1024]{1,0:T(8,128)(2,1)S(1)} collective-permute-done((bf16[512,1024]{1,0:T(8,128)(2,1)S(1)}, bf16[512,1024]{1,0:T(8,128)(2,1)S(1)}, u32[]{:S(2)}, u32[]{:S(2)}) %collective-permute-start.3) | collective-permute-done | bytes 1048608 | tf_op jit(solution)/shard_map/ppermute | solution.py:542
  392.9 142.5 %shard_map.254 = (bf16[8,2,64,1536]{3,2,1,0:T(8,128)(2,1)}, bf16[8,96,1024]{2,1,0:T(8,128)(2,1)}, bf16[8,64,1024]{2,1,0:T(8,128)(2,1)}, bf16[8,256,512]{2,1,0:T(8,128)(2,1)}) custom-call(bf16[4,2,64,1536]{3,2,1,0:T(8,128)(2,1)} %bitcast.223, bf16[4,96,1024]{2,1,0:T(8,128)(2,1)} %bitcast.229, bf16[8,64,1024]{2,1,0:T(8,128)(2,1)} %bitcast.226, ...), custom_call_target="tpu_custom_call" | custom-call | tf_op jit(solution)/shard_map/pallas_call | solution.py:747
  539.9 6.4 %reshape.395 = bf16[4,2,2,64,2,2,384]{6,5,4,3,2,1,0:T(2,128)(2,1)S(1)} reshape(bf16[8,2,64,1536]{3,2,1,0:T(8,128)(2,1)} %get-tuple-element.29) | data formatting | bytes 6291456 | tf_op jit(solution)/shard_map/reshape | solution.py:1257
  551.6 3.7 reshape.407
  555.3 4.3 copy.157
  (262 shorter events, 127.3 us)
Async XLA Ops:
  7.2 8.8 %copy-start = (bf16[768,1024]{1,0:T(8,128)(2,1)S(1)}, bf16[768,1024]{1,0:T(8,128)(2,1)}, u32[]{:S(2)}) copy-start(bf16[768,1024]{1,0:T(8,128)(2,1)} %param.28) | copy-start | bytes 4718596
  7.2 114.1 %all-gather.4.cloned.1.call-start = ((), (), s32[]{:S(2)}) async-start(), calls=%async_computation.1 | async-start | bytes 5242880 | tf_op jit(solution)/shard_map/all_gather | solution.py:538
  7.9 130.5 %all-gather.6.cloned.1.call-start = ((), (), s32[]{:S(2)}) async-start(), calls=%async_computation.2 | async-start | bytes 4718592 | tf_op jit(solution)/shard_map/all_gather | solution.py:1163
  15.9 128.9 %all-gather.8.cloned.1.call-start = ((), (), s32[]{:S(2)}) async-start(), calls=%async_computation.3 | async-start | bytes 2359296 | tf_op jit(solution)/shard_map/all_gather | solution.py:1165
  66.6 177.4 %copy-start.2 = (f32[1280,512]{0,1:T(8,128)}, f32[1280,512]{0,1:T(8,128)S(1)}, u32[]{:S(2)}) copy-start(f32[1280,512]{0,1:T(8,128)S(1)} %fusion.73) | copy-start | bytes 7864324
  78.3 4.8 copy-start.4
  107.5 17.0 %copy-start.10 = (bf16[8,20,8,256]{3,2,0,1:T(8,128)(2,1)}, bf16[8,20,8,256]{3,2,0,1:T(8,128)(2,1)S(1)}, u32[]{:S(2)}) copy-start(bf16[8,20,8,256]{3,2,0,1:T(8,128)(2,1)S(1)} %copy.177) | copy-start | bytes 1966084
  144.9 6.2 %copy-start.49 = (bf16[768,1024]{1,0:T(8,128)(2,1)S(1)}, bf16[768,1024]{1,0:T(8,128)(2,1)}, u32[]{:S(2)}) copy-start(bf16[768,1024]{1,0:T(8,128)(2,1)} %all-gather.8.cloned.1.call-done) | copy-start | bytes 4718596
  151.1 16.2 %copy-start.48 = (bf16[4,256,1536]{2,1,0:T(8,128)(2,1)S(1)}, bf16[4,256,1536]{2,1,0:T(8,128)(2,1)}, u32[]{:S(2)}) copy-start(bf16[4,256,1536]{2,1,0:T(8,128)(2,1)} %all-gather.6.cloned.1.call-done) | copy-start | bytes 9437188
  172.0 14.7 %copy-start.30 = (f32[160,1024]{1,0:T(8,128)S(1)}, f32[160,1024]{1,0:T(8,128)}, u32[]{:S(2)}) copy-start(f32[160,1024]{1,0:T(8,128)} %shard_map.249) | copy-start | bytes 1966084
  172.0 14.7 %copy-start.40 = (bf16[1,160,1024]{2,1,0:T(8,128)(2,1)S(1)}, bf16[1,160,1024]{2,1,0:T(8,128)(2,1)}, u32[]{:S(2)}) copy-start(bf16[1,160,1024]{2,1,0:T(8,128)(2,1)} %param.29) | copy-start | bytes 983044
  189.9 4.6 copy-start.38
  244.0 7.2 %copy-start.23 = (f32[1280,64]{0,1:T(8,128)S(1)}, f32[1280,64]{0,1:T(8,128)}, u32[]{:S(2)}) copy-start(f32[1280,64]{0,1:T(8,128)} %copy-done.22) | copy-start | bytes 983044
  244.0 7.2 %copy-start.27 = (bf16[1280,2,128]{0,2,1:T(8,128)(2,1)S(1)}, bf16[1280,2,128]{0,2,1:T(8,128)(2,1)}, u32[]{:S(2)}) copy-start(bf16[1280,2,128]{0,2,1:T(8,128)(2,1)} %copy-done.26) | copy-start | bytes 1966084
  262.0 98.5 %collective-permute-start.4 = (bf16[2,256,512]{2,1,0:T(8,128)(2,1)}, bf16[2,256,512]{2,1,0:T(8,128)(2,1)}, u32[]{:S(2)}, u32[]{:S(2)}) collective-permute-start(bf16[2,256,512]{2,1,0:T(8,128)(2,1)} %dynamic-slice_bitcast_fusion.4), channel_id=1, source_target_pairs={{0,1},{1,0},{2,3},{3,2},{4,5},{5,4},{6,7},{7,6},{8,9},{9,8},{10,11... | collective-permute-start | bytes 1572872 | tf_op jit(solution)/shard_map/ppermute | solution.py:542
  263.5 100.7 %collective-permute-start.2 = (bf16[2,512,1024]{2,1,0:T(8,128)(2,1)}, bf16[2,512,1024]{2,1,0:T(8,128)(2,1)S(1)}, u32[]{:S(2)}, u32[]{:S(2)}) collective-permute-start(bf16[2,512,1024]{2,1,0:T(8,128)(2,1)} %dynamic-slice_bitcast_fusion), channel_id=1, source_target_pairs={{0,1},{1,0},{2,3},{3,2},{4,5},{5,4},{6,7},{7,6},{8,9},{9,8},{10,11... | collective-permute-start | bytes 6291464 | tf_op jit(solution)/shard_map/ppermute | solution.py:542
  264.9 107.2 %collective-permute-start.1 = (bf16[384,1024]{1,0:T(8,128)(2,1)}, bf16[384,1024]{1,0:T(8,128)(2,1)}, u32[]{:S(2)}, u32[]{:S(2)}) collective-permute-start(bf16[384,1024]{1,0:T(8,128)(2,1)} %dynamic-slice_bitcast_fusion.3), channel_id=1, source_target_pairs={{0,2},{2,0},{1,3},{3,1},{4,6},{6,4},{5,7},{7,5},{8,10},{10,8},{9,1... | collective-permute-start | bytes 2359304 | tf_op jit(solution)/shard_map/ppermute | solution.py:542
  267.6 106.8 %collective-permute-start = (bf16[512,1536]{1,0:T(8,128)(2,1)}, bf16[512,1536]{1,0:T(8,128)(2,1)}, u32[]{:S(2)}, u32[]{:S(2)}) collective-permute-start(bf16[512,1536]{1,0:T(8,128)(2,1)} %dynamic-slice_bitcast_fusion.1), channel_id=1, source_target_pairs={{0,2},{2,0},{1,3},{3,1},{4,6},{6,4},{5,7},{7,5},{8,10},{10,8},{9,1... | collective-permute-start | bytes 4718600 | tf_op jit(solution)/shard_map/ppermute | solution.py:542
  271.2 37.6 %copy-start.17 = (bf16[1,160,1024]{2,1,0:T(8,128)(2,1)S(1)}, bf16[1,160,1024]{2,1,0:T(8,128)(2,1)}, u32[]{:S(2)}) copy-start(bf16[1,160,1024]{2,1,0:T(8,128)(2,1)} %param.15) | copy-start | bytes 983044
  308.8 50.6 %copy-start.13 = (f32[160,1024]{1,0:T(8,128)S(1)}, f32[160,1024]{1,0:T(8,128)}, u32[]{:S(2)}) copy-start(f32[160,1024]{1,0:T(8,128)} %shard_map.253) | copy-start | bytes 1966084
  361.8 9.6 %collective-permute-start.5 = (bf16[256,512]{1,0:T(8,128)(2,1)S(1)}, bf16[256,512]{1,0:T(8,128)(2,1)S(1)}, u32[]{:S(2)}, u32[]{:S(2)}) collective-permute-start(bf16[256,512]{1,0:T(8,128)(2,1)S(1)} %dynamic-slice_bitcast_fusion.5), channel_id=1, source_target_pairs={{0,2},{2,0},{1,3},{3,1},{4,6},{6,4},{5,7},{7,5},{8,10},{10,8},{9,1... | collective-permute-start | bytes 786440 | tf_op jit(solution)/shard_map/ppermute | solution.py:542
  366.7 5.4 copy-start.37
  366.8 7.7 %copy-start.21 = (bf16[1024,1536]{1,0:T(8,128)(2,1)S(1)}, bf16[1024,1536]{1,0:T(8,128)(2,1)}, u32[]{:S(2)}) copy-start(bf16[1024,1536]{1,0:T(8,128)(2,1)} %convolution_convert_fusion) | copy-start | bytes 9437188
  366.8 24.8 %collective-permute-start.3 = (bf16[512,1024]{1,0:T(8,128)(2,1)S(1)}, bf16[512,1024]{1,0:T(8,128)(2,1)S(1)}, u32[]{:S(2)}, u32[]{:S(2)}) collective-permute-start(bf16[512,1024]{1,0:T(8,128)(2,1)S(1)} %dynamic-slice_bitcast_fusion.2), channel_id=1, source_target_pairs={{0,2},{2,0},{1,3},{3,1},{4,6},{6,4},{5,7},{7,5},{8,10},{10,8},{9,1... | collective-permute-start | bytes 3145736 | tf_op jit(solution)/shard_map/ppermute | solution.py:542
  (43 other events, 113.7 us)
Sparse Core Ops, SparseCore 0:
  9.6 40.0 all-gather.3
  51.3 46.9 all-gather.5
  100.3 27.1 all-gather.7

commit v3 on v2

--- a/solution.py
+++ b/solution.py
@@ -501,7 +501,7 @@
 
 CTX = ("z", "y")
 FSDP = ("x", "core")
-VMEM_BYTES = 56 << 20
+VMEM_BYTES = 62 << 20
 
 
 def norm_back(values, gain_vec, grad):
@@ -937,116 +937,476 @@
     return [pltpu.VMEM((LINE, rows, cols), jnp.float32), line, line, line, line]
 
 
-def sum_sides(net, src, from_side, line):
+def sum_sides(net, src, from_side, line, make=None):
     z, y = net.z, net.y
     held = line[0]
     order = far_first(z)
-    sides = [net.put(src.at[2 * k + 1 - y], from_side.at[k], net.at(dy=1)) for k in order]
+    sides = []
+    for k in order:
+        if make is not None:
+            make(2 * k + 1 - y)
+        sides.append(net.put(src.at[2 * k + 1 - y], from_side.at[k], net.at(dy=1)))
 
     def ready(t):
         k = order[t]
+        if make is not None:
+            make(2 * k + y)
         sides[t].arrived()
         held[k] = src[2 * k + y].astype(jnp.float32) + from_side[k].astype(jnp.float32)
 
     yield from sum_line(net, *line, ready)
 
 
-def scatter_ctx(parts, number):
-    _, rows, cols = parts.shape
-
-    def body(net, local, src, out, from_side, *line):
-        greet(net, ("z", "y"))
-        drive(sum_sides(net, src, from_side, line))
-        out[...] = line[0][net.z]
-        net.close()
-
-    return net_call(
-        body,
-        [shape_of(rows, cols, kind=jnp.float32)],
-        [parts],
-        12,
-        0,
-        number,
-        scratch=[pltpu.VMEM((LINE, rows, cols), jnp.bfloat16)] + line_scratch(rows, cols),
-        vmem=(0, 1),
-    )[0]
-
-
-def sum_and_gather(gate_up, down, out_proj, heads, number):
-    _, _, gu_rows, gu_cols = gate_up.shape
-    dn_rows, dn_cols = down.shape[1:]
-    o_rows, o_cols = out_proj.shape[1:]
-
-    def body(net, local, gu, dn, op, hd, gu_all, dn_all, op_all, hd_all, *scratch):
-        gu_line, dn_line, op_line = scratch[:5], scratch[5:10], scratch[10:15]
-        op_side, gu_low, gu_pair, dn_low, op_low = scratch[15:]
-        greet(net, ("z", "y", "core"))
-        z, core = net.z, net.core
-        mine = own_copies([(hd, hd_all.at[net.me])], local)
-
-        def gu_ready(t):
-            k = far_first(z)[t]
-            for c in range(2):
-                gu_line[0][k, pl.ds(c * gu_rows, gu_rows)] = gu[k, c].astype(jnp.float32)
-
-        def dn_ready(t):
-            k = far_first(z)[t]
-            dn_line[0][k] = dn[k].astype(jnp.float32)
-
-        drive(
-            sum_line(net, *gu_line, gu_ready),
-            sum_line(net, *dn_line, dn_ready),
-            sum_sides(net, op, op_side, op_line),
-        )
-        dn_low[...] = low(dn_line[0][z])
-        op_low[...] = low(op_line[0][z])
-        for c in range(2):
-            gu_low[c] = low(gu_line[0][z, pl.ds(c * gu_rows, gu_rows)])
-        swap = net.put(gu_low.at[1 - core], gu_pair.at[core], net.at(dc=1))
-        gu_pair[core] = gu_low[core]
-        swap.arrived()
-        rest = own_copies(
-            [
-                (gu_pair, gu_all.at[net.me]),
-                (dn_low, dn_all.at[net.me]),
-                (op_low, op_all.at[net.me]),
-            ],
-            local.at[pl.ds(1, 3)],
-        )
-        drive(
-            gather_line_first(net, gu_pair, lambda slot: gu_all.at[slot]),
-            gather_line_first(net, dn_low, lambda slot: dn_all.at[slot]),
-            gather_line_first(net, op_low, lambda slot: op_all.at[slot]),
-            gather_side_first(net, hd, lambda slot: hd_all.at[slot]),
-        )
-        for copy in mine + rest:
-            copy.wait()
-        net.close()
-
-    return net_call(
-        body,
-        [
-            shape_of(2 * LINE, 2, gu_rows, gu_cols),
-            shape_of(2 * LINE, dn_rows, dn_cols),
-            shape_of(2 * LINE, o_rows, o_cols),
-            shape_of(2 * LINE, *heads.shape),
+BLOCK = 256
+
+
+def turn_lanes(v):
+    return pltpu.roll(v, HEAD_SIZE // 2, 1)
+
+
+def dot_last(a, b):
+    return lax.dot_general(a, b, (((1,), (1,)), ((), ())), preferred_element_type=jnp.float32)
+
+
+def resting(rounds):
+    for _ in range(rounds):
+        yield
+
+
+class Bag:
+    def __init__(self, **members):
+        self.__dict__.update(members)
+
+
+def bags(tree):
+    return Bag(**{n: bags(v) for n, v in tree.items()}) if isinstance(tree, dict) else tree
+
+
+def back_kernel(dims, number):
+    rows, count, piece_rows = dims
+    blocks = count // BLOCK
+    scale = HEAD_SIZE**-0.5
+    width = 2 * HEAD_SIZE
+    d = MODEL_WIDTH
+
+    def run(moved, loaded):
+        a = Bag(**moved)
+        gu_rows, gu_cols = a.gate.shape[1:]
+        dn_rows = a.down.shape[1]
+        o_rows = a.oproj.shape[1]
+        bf, f32 = jnp.bfloat16, jnp.float32
+        z_gu, z_dn, z_o = gu_rows // LINE, dn_rows // LINE, o_rows // (2 * LINE)
+        gain_width = 2 * d + 2 * HEAD_SIZE
+
+        def quarter():
+            return dict(
+                own=pltpu.VMEM((2, gu_rows, gu_cols), bf),
+                got=pltpu.VMEM((2, gu_rows, gu_cols), bf),
+                low=pltpu.VMEM((2, z_gu, gu_cols), bf),
+                pair=pltpu.VMEM((2, z_gu, gu_cols), bf),
+                line=line_scratch(2 * z_gu, gu_cols),
+            )
+
+        scratch = dict(
+            held={n: pltpu.VMEM(v.shape, v.dtype) for n, v in loaded.items()},
+            gate=quarter(),
+            up=quarter(),
+            down=dict(
+                own=pltpu.VMEM((dn_rows, d), bf),
+                got=pltpu.VMEM((dn_rows, d), bf),
+                low=pltpu.VMEM((z_dn, d), bf),
+                line=line_scratch(z_dn, d),
+            ),
+            o=dict(
+                own=pltpu.VMEM((2, o_rows, d), bf),
+                core=pltpu.VMEM((2, o_rows, d), bf),
+                got=pltpu.VMEM((o_rows, d), bf),
+                sum=pltpu.VMEM((2 * LINE, z_o, d), bf),
+                side=pltpu.VMEM((LINE, z_o, d), bf),
+                low=pltpu.VMEM((z_o, d), bf),
+                line=line_scratch(z_o, d),
+            ),
+            h=dict(
+                own=pltpu.VMEM((4, d // 4, 2 * width), bf),
+                core=pltpu.VMEM((2, d // 4, 2 * width), bf),
+                got=pltpu.VMEM((d // 4, 2 * width), bf),
+                low=pltpu.VMEM((d // 4, 2 * width), bf),
+            ),
+            dm_all=pltpu.VMEM((2 * LINE, rows, width), bf),
+            do=pltpu.VMEM((count, width), bf),
+            dk=pltpu.VMEM((count, HEAD_SIZE), f32),
+            dv=pltpu.VMEM((count, HEAD_SIZE), f32),
+            dqkv=pltpu.VMEM((count, 2 * width), bf),
+            dgq=pltpu.VMEM((1, HEAD_SIZE), f32),
+            dgk=pltpu.VMEM((1, HEAD_SIZE), f32),
+            part=dict(
+                sum=pltpu.VMEM((2 * LINE, rows, d), bf),
+                side=pltpu.VMEM((LINE, rows, d), bf),
+                line=line_scratch(rows, d),
+            ),
+            g=dict(
+                mine=pltpu.VMEM((1, gain_width), f32),
+                pair=pltpu.VMEM((1, gain_width), f32),
+                four=pltpu.VMEM((1, gain_width), f32),
+                got=pltpu.VMEM((2, 1, gain_width), f32),
+                all=pltpu.VMEM((2 * LINE, 1, gain_width), f32),
+            ),
+        )
+        flat, tree = jax.tree.flatten(scratch)
+        f_in, in_tree = jax.tree.flatten((moved, loaded))
+        outs = dict(
+            dx1=shape_of(rows, d, kind=f32),
+            back=shape_of(*a.back.shape),
+            gains=shape_of(1, gain_width, kind=f32),
+            gate=shape_of(2 * LINE, 2, z_gu, gu_cols),
+            up=shape_of(2 * LINE, 2, z_gu, gu_cols),
+            down=shape_of(2 * LINE, z_dn, d),
+            o=shape_of(2 * LINE, z_o, d),
+            heads=shape_of(2 * LINE, d // 4, 2 * width),
+        )
+        f_out, out_tree = jax.tree.flatten(outs)
+
+        def body(net, local, *refs):
+            given, to_load = jax.tree.unflatten(in_tree, refs[: len(f_in)])
+            given = Bag(**given)
+            out = Bag(**jax.tree.unflatten(out_tree, refs[len(f_in) : len(f_in) + len(f_out)]))
+            r = bags(jax.tree.unflatten(tree, refs[len(f_in) + len(f_out) :]))
+            h = r.held
+            z, y, x, core, me = net.z, net.y, net.x, net.core, net.me
+            slots = 2 * LINE
+            used = iter(range(64))
+
+            def fetch(src, dst):
+                copy = pltpu.make_async_copy(src, dst, local.at[next(used)])
+                copy.start()
+                return copy
+
+            greet(net, ("ctx", "x", "core"))
+            done = set()
+            dm_own = fetch(given.dm.at[me], r.dm_all.at[me])
+            for k in range(1, slots):
+                other = lax.rem(me + k, slots)
+                there = (other // 2, lax.rem(other, 2), x, core)
+                net.put(given.dm.at[other], r.dm_all.at[me], there)
+            dm_copies = list(net.open)
+            loads = [fetch(to_load[n], getattr(h, n)) for n in to_load]
+
+            def over_x(src, piece):
+                own = [fetch(src.at[2 * x + c], piece.own.at[c]) for c in range(2)]
+                sent = [
+                    net.put(src.at[2 * (1 - x) + c], piece.got.at[c], net.at(dx=1))
+                    for c in range(2)
+                ]
+                return own, sent
+
+            o_own = [fetch(given.oproj.at[2 * s + core], r.o.own.at[s]) for s in range(2)]
+            o_core = [
+                net.put(given.oproj.at[2 * s + 1 - core], r.o.core.at[s], net.at(dc=1))
+                for s in range(2)
+            ]
+            gate_over, up_over = over_x(given.gate, r.gate), over_x(given.up, r.up)
+            down_over = (
+                [fetch(given.down.at[x], r.down.own)],
+                [net.put(given.down.at[1 - x], r.down.got, net.at(dx=1))],
+            )
+
+            def land(over):
+                own, sent = over
+                for c in own:
+                    c.wait()
+                for c in sent:
+                    c.arrived()
+
+            def main():
+                for c in loads:
+                    c.wait()
+                dm_own.wait()
+                for c in dm_copies:
+                    c.arrived()
+                yield
+                for i in range(blocks):
+                    t = i * BLOCK + lax.broadcasted_iota(jnp.int32, (BLOCK, count), 0)
+                    hot = low(jnp.where(h.dealt[...] == t, 1.0, 0.0))
+                    r.do[pl.ds(i * BLOCK, BLOCK)] = low(
+                        dot(hot, r.dm_all[...].reshape(count, width))
+                    )
+                r.dk[...] = jnp.zeros_like(r.dk)
+                r.dv[...] = jnp.zeros_like(r.dv)
+                yield
+                dgq = jnp.zeros((1, HEAD_SIZE), f32)
+                for i in range(blocks):
+                    here = pl.ds(i * BLOCK, BLOCK)
+                    first = h.first[:, here]
+                    t = i * BLOCK + lax.broadcasted_iota(jnp.int32, (BLOCK, BLOCK), 1)
+                    heads = []
+                    for g in range(2):
+                        lanes = pl.ds(g * HEAD_SIZE, HEAD_SIZE)
+                        q, do = h.q[here, lanes], r.do[here, lanes]
+                        product = do.astype(f32) * h.mixed[here, lanes]
+                        delta = jnp.sum(jnp.transpose(product), axis=0, keepdims=True)
+                        heads.append((q, do, h.lse[g, :, here], delta))
+
+                    def step(j, held, heads=heads, first=first, t=t):
+                        at = pl.ds(pl.multiple_of(j * BLOCK, BLOCK), BLOCK)
+                        k, v, kt = h.k[at], h.v[at], h.kt[:, at]
+                        u = j * BLOCK + lax.broadcasted_iota(jnp.int32, (BLOCK, BLOCK), 0)
+                        allowed = (u >= first) & (u <= t)
+                        dk, dv, out = r.dk[at], r.dv[at], []
+                        for (q, do, lse, delta), dq in zip(heads, held):
+                            p = jnp.where(allowed, jnp.exp(dot_last(k, q) * scale - lse), 0.0)
+                            ds = low(p * (dot_last(v, do) - delta))
+                            dv = dv + dot(low(p), do)
+                            dk = dk + dot(ds, q)
+                            out.append(dq + dot(kt, ds))
+                        r.dk[at] = dk
+                        r.dv[at] = dv
+                        return tuple(out)
+
+                    zero = jnp.zeros((HEAD_SIZE, BLOCK), f32)
+                    result = lax.fori_loop(0, i + 1, step, (zero, zero))
+                    cos, sin = h.cos[here], h.sin[here]
+                    for g in range(2):
+                        lanes = pl.ds(g * HEAD_SIZE, HEAD_SIZE)
+                        grad = jnp.transpose(result[g]) * scale
+                        grad = grad * cos - turn_lanes(grad) * sin
+                        dx, dg = norm_back(h.q_pre[here, lanes], h.q_gain[...], grad)
+                        r.dqkv[here, lanes] = low(dx)
+                        dgq = dgq + jnp.sum(dg, axis=0, keepdims=True)
+                    yield
+                dgk = jnp.zeros((1, HEAD_SIZE), f32)
+                for i in range(blocks):
+                    here = pl.ds(i * BLOCK, BLOCK)
+                    grad = r.dk[here] * scale
+                    grad = grad * h.cos[here] - turn_lanes(grad) * h.sin[here]
+                    dx, dg = norm_back(h.k_pre[here], h.k_gain[...], grad)
+                    r.dqkv[here, pl.ds(width, HEAD_SIZE)] = low(dx)
+                    r.dqkv[here, pl.ds(width + HEAD_SIZE, HEAD_SIZE)] = low(r.dv[here])
+                    dgk = dgk + jnp.sum(dg, axis=0, keepdims=True)
+                r.dgq[...] = dgq
+                r.dgk[...] = dgk
+                done.add("dqkv")
+
+                def make(slot):
+                    at = pl.ds(pl.multiple_of(slot * rows, rows), rows)
+                    r.part.sum[slot] = low(dot_last(r.dqkv[at], h.w_qkv[...]))
+
+                yield from sum_sides(net, r.part.sum, r.part.side, r.part.line, make)
+                dx1, dg1 = norm_back(
+                    h.tok[...].astype(f32), h.a_gain[...], r.part.line[0][z]
+                )
+                out.dx1[...] = dx1
+                r.g.mine[:, pl.ds(0, d)] = jnp.sum(dg1, axis=0, keepdims=True)
+                r.g.mine[:, pl.ds(d, d)] = h.dg2[...]
+                r.g.mine[:, pl.ds(2 * d, HEAD_SIZE)] = r.dgq[...]
+                r.g.mine[:, pl.ds(2 * d + HEAD_SIZE, HEAD_SIZE)] = r.dgk[...]
+                done.add("gains")
+                yield
+
+            def gains():
+                while "gains" not in done:
+                    yield
+                pair = net.put(r.g.mine, r.g.got.at[0], net.at(dc=1))
+                yield
+                pair.arrived()
+                r.g.pair[...] = r.g.mine[...] + r.g.got[0]
+                four = net.put(r.g.pair, r.g.got.at[1], net.at(dx=1))
+                yield
+                four.arrived()
+                r.g.four[...] = r.g.pair[...] + r.g.got[1]
+                r.g.all[me] = r.g.four[...]
+                copies = []
+                for k in range(1, slots):
+                    other = lax.rem(me + k, slots)
+                    there = (other // 2, lax.rem(other, 2), x, core)
+                    copies.append(net.put(r.g.four, r.g.all.at[me], there))
+                yield
+                yield
+                for c in copies:
+                    c.arrived()
+                out.gains[...] = jnp.sum(r.g.all[...], axis=0)
+                yield
+
+            def back_rows():
+                while "dqkv" not in done:
+                    yield
+                own = fetch(given.back.at[me], out.back.at[me])
+                for k in range(1, slots):
+                    other = lax.rem(me + k, slots)
+                    there = (other // 2, lax.rem(other, 2), x, core)
+                    net.put(given.back.at[other], out.back.at[me], there)
+                yield
+                own.wait()
+
+            def gate_or_up(over, piece, gathered, rest):
+                yield from resting(rest)
+                land(over)
+                line = piece.line
+
+                def ready(t):
+                    k = far_first(z)[t]
+                    at = pl.ds(pl.multiple_of(k * z_gu, z_gu), z_gu)
+                    for c in range(2):
+                        line[0][k, pl.ds(c * z_gu, z_gu)] = piece.own[c, at].astype(
+                            f32
+                        ) + piece.got[c, at].astype(f32)
+
+                yield from sum_line(net, *line, ready)
+                for c in range(2):
+                    piece.low[c] = low(line[0][z, pl.ds(c * z_gu, z_gu)])
+                swap = net.put(piece.low.at[1 - core], piece.pair.at[core], net.at(dc=1))
+                piece.pair[core] = piece.low[core]
+                yield
+                swap.arrived()
+                own = fetch(piece.pair, gathered.at[me])
+                yield from gather_line_first(net, piece.pair, lambda slot: gathered.at[slot])
+                own.wait()
+
+            def down(rest):
+                yield from resting(rest)
+                land(down_over)
+                line = r.down.line
+
+                def ready(t):
+                    k = far_first(z)[t]
+                    at = pl.ds(pl.multiple_of(k * z_dn, z_dn), z_dn)
+                    line[0][k] = r.down.own[at].astype(f32) + r.down.got[at].astype(f32)
+
+                yield from sum_line(net, *line, ready)
+                r.down.low[...] = low(line[0][z])
+                own = fetch(r.down.low, out.down.at[me])
+                yield from gather_line_first(net, r.down.low, lambda slot: out.down.at[slot])
+                own.wait()
+
+            def out_proj(rest_core, rest_x):
+                yield from resting(rest_core)
+                for c in o_own:
+                    c.wait()
+                for c in o_core:
+                    c.arrived()
+                r.o.own[...] = low(r.o.own[...].astype(f32) + r.o.core[...].astype(f32))
+                over = net.put(r.o.own.at[1 - x], r.o.got, net.at(dx=1))
+                yield from resting(rest_x)
+                over.arrived()
+                for i in range(slots):
+                    at = pl.ds(i * z_o, z_o)
+                    r.o.sum[i] = low(r.o.own[x, at].astype(f32) + r.o.got[at].astype(f32))
+                yield from sum_sides(net, r.o.sum, r.o.side, r.o.line)
+                r.o.low[...] = low(r.o.line[0][z])
+                own = fetch(r.o.low, out.o.at[me])
+                yield from gather_line_first(net, r.o.low, lambda slot: out.o.at[slot])
+                own.wait()
+
+            def heads(rest):
+                while "dqkv" not in done:
+                    yield
+                for f in range(4):
+                    at = pl.ds(f * (d // 4), d // 4)
+                    r.h.own[f] = low(outer_rows(h.normed[:, at], r.dqkv[...]))
+                core_copies = [
+                    net.put(r.h.own.at[2 * s + 1 - core], r.h.core.at[s], net.at(dc=1))
+                    for s in range(2)
+                ]
+                yield
+                for c in core_copies:
+                    c.arrived()
+                for s in range(2):
+                    f = 2 * s + core
+                    r.h.own[f] = low(r.h.own[f].astype(f32) + r.h.core[s].astype(f32))
+                over = net.put(r.h.own.at[2 * (1 - x) + core], r.h.got, net.at(dx=1))
+                yield from resting(rest)
+                over.arrived()
+                r.h.low[...] = low(
+                    r.h.own[2 * x + core].astype(f32) + r.h.got[...].astype(f32)
+                )
+                own = fetch(r.h.low, out.heads.at[me])
+                yield from gather_line_first(net, r.h.low, lambda slot: out.heads.at[slot])
+                own.wait()
+
+            drive(
+                main(),
+                gate_or_up(gate_over, r.gate, out.gate, 3),
+                gate_or_up(up_over, r.up, out.up, 9),
+                down(11),
+                out_proj(1, 13),
+                heads(3),
+                back_rows(),
+                gains(),
+            )
+            net.close()
+
+        order = jax.tree.unflatten(out_tree, range(len(f_out)))
+        result = net_call(
+            body,
+            f_out,
+            f_in,
+            200,
+            64,
+            number,
+            scratch=flat,
+            vmem=(len(f_in) + order.get("dx1"), len(f_in) + order.get("gains")),
+        )
+        return Bag(**jax.tree.unflatten(out_tree, result))
+
+    return run
+
+
+def widen(gate_all, up_all, down_all, o_all, heads_all):
+    _, _, z_gu, gu_cols = gate_all.shape
+    half = gu_cols // 2
+    z_dn, z_o = down_all.shape[1], o_all.shape[1]
+    h_rows = heads_all.shape[1] // LINE
+
+    def kernel(gate, up, down, o, heads, gate_out, up_out, down_out, o_out, q_out, k_out, v_out):
+        for src, out in ((gate, gate_out), (up, up_out)):
+            for y in range(2):
+                for c in range(2):
+                    for xs in range(2):
+                        to = (2 * xs + c) * 2 * half + y * half
+                        out[:, pl.ds(to, half)] = src[y, c, :, pl.ds(xs * half, half)].astype(
+                            jnp.float32
+                        )
+        for y in range(2):
+            down_out[y] = down[y].astype(jnp.float32)
+            o_out[pl.ds(y * z_o, z_o)] = o[y].astype(jnp.float32)
+        for h in range(2 * LINE):
+            q_out[:, pl.ds(h * 256, 256)] = heads[h, :, pl.ds(0, 256)].astype(jnp.float32)
+            k_out[:, pl.ds(h * 128, 128)] = heads[h, :, pl.ds(256, 128)].astype(jnp.float32)
+            v_out[:, pl.ds(h * 128, 128)] = heads[h, :, pl.ds(384, 128)].astype(jnp.float32)
+
+    f32 = jnp.float32
+    outs = pl.pallas_call(
+        kernel,
+        grid=(LINE,),
+        in_specs=[
+            pl.BlockSpec((2, 2, z_gu, gu_cols), lambda i: (i, 0, 0, 0)),
+            pl.BlockSpec((2, 2, z_gu, gu_cols), lambda i: (i, 0, 0, 0)),
+            pl.BlockSpec((2, z_dn, MODEL_WIDTH), lambda i: (i, 0, 0)),
+            pl.BlockSpec((2, z_o, MODEL_WIDTH), lambda i: (i, 0, 0)),
+            pl.BlockSpec((2 * LINE, h_rows, 512), lambda i: (0, i, 0)),
         ],
-        [gate_up, down, out_proj, heads],
-        96,
-        4,
-        number,
-        scratch=line_scratch(2 * gu_rows, gu_cols)
-        + line_scratch(dn_rows, dn_cols)
-        + line_scratch(o_rows, o_cols)
-        + [
-            pltpu.VMEM((LINE, o_rows, o_cols), jnp.bfloat16),
-            pltpu.VMEM((2, gu_rows, gu_cols), jnp.bfloat16),
-            pltpu.VMEM((2, gu_rows, gu_cols), jnp.bfloat16),
-            pltpu.VMEM((dn_rows, dn_cols), jnp.bfloat16),
-            pltpu.VMEM((o_rows, o_cols), jnp.bfloat16),
+        out_specs=[
+            pl.BlockSpec((z_gu, 8 * half), lambda i: (i, 0)),
+            pl.BlockSpec((z_gu, 8 * half), lambda i: (i, 0)),
+            pl.BlockSpec((2, z_dn, MODEL_WIDTH), lambda i: (0, i, 0)),
+            pl.BlockSpec((2 * z_o, MODEL_WIDTH), lambda i: (i, 0)),
+            pl.BlockSpec((h_rows, 2048), lambda i: (i, 0)),
+            pl.BlockSpec((h_rows, 1024), lambda i: (i, 0)),
+            pl.BlockSpec((h_rows, 1024), lambda i: (i, 0)),
         ],
-        vmem=(0, 1, 2),
-    )
+        out_shape=[
+            shape_of(LINE * z_gu, 8 * half, kind=f32),
+            shape_of(LINE * z_gu, 8 * half, kind=f32),
+            shape_of(2, LINE * z_dn, MODEL_WIDTH, kind=f32),
+            shape_of(2 * LINE * z_o, MODEL_WIDTH, kind=f32),
+            shape_of(LINE * h_rows, 2048, kind=f32),
+            shape_of(LINE * h_rows, 1024, kind=f32),
+            shape_of(LINE * h_rows, 1024, kind=f32),
+        ],
+        compiler_params=pltpu.CompilerParams(vmem_limit_bytes=VMEM_BYTES),
+    )(gate_all, up_all, down_all, o_all, heads_all)
+    outs = list(outs)
+    outs[2] = outs[2].reshape(-1, MODEL_WIDTH)
+    return outs
 
 
 def fast_layer(
@@ -1180,101 +1540,74 @@
     d_gu = jnp.concatenate([d_gate, d_up], axis=1)
     dn2_part = low(dot_trans(d_gu, w_gu))
     d_normed2 = scatter_four(dn2_part.reshape(4, rows, -1), 5)
-    grad_gu = low(outer_rows(quad_n, d_gu))
+    grad_gate = low(outer_rows(quad_n, d_gate))
+    grad_up = low(outer_rows(quad_n, d_up))
     grad_dn = low(outer_rows(hidden, quad_g))
     dx2, dg2 = norm_back(middle, m_gain, d_normed2)
     d_middle = out_cotangent[0].astype(jnp.float32) + dx2
     middle_low = low(d_middle)
     d_mixed_tok = low(dot_trans(middle_low, full_o))
     dm_out = jnp.transpose(d_mixed_tok.reshape(rows, slots, width), (1, 0, 2))
-    padded = jnp.pad(
-        middle_low.reshape(slots, piece, MODEL_WIDTH), ((0, 0), (0, 32 - piece), (0, 0))
-    )
-    dm_in, back = swap_two(dm_out, padded, 6)
-    dm_in = dm_in.reshape(count, width)
-    d_mixed = low(
-        lax.dot_general(
-            to_dealt, dm_in, (((0,), (0,)), ((), ())), preferred_element_type=jnp.float32
-        )
-    )
     grad_o = low(outer_rows(mixed_low, middle_low))
-    d_heads = d_mixed.reshape(count, 2, HEAD_SIZE)
-    delta = jnp.sum(
-        jnp.transpose(d_heads, (1, 0, 2)).astype(jnp.float32) * mixed, axis=-1, keepdims=True
-    )
-    probs = jnp.where(allowed, jnp.exp(scores - log_total), 0.0)
-    d_probs = jnp.einsum("tgh,uh->gtu", d_heads, v_low, preferred_element_type=jnp.float32)
-    d_scores = low(probs * (d_probs - delta))
-    d_v = jnp.einsum("gtu,tgh->uh", low(probs), d_heads, preferred_element_type=jnp.float32)
-    d_q = jnp.einsum("gtu,uh->tgh", d_scores, k_low, preferred_element_type=jnp.float32) * scale
-    d_k = jnp.einsum("gtu,tgh->uh", d_scores, q_low, preferred_element_type=jnp.float32) * scale
-
-    def rope_back(v, cos, sin):
-        return v * cos - half_turn(v * sin)
-
-    d_q_pre, dg_q = norm_back(q_pre, q_gain, rope_back(d_q, cosine[:, None], sine[:, None]))
-    d_k_pre, dg_k = norm_back(k_pre, k_gain_all, rope_back(d_k, cosine, sine))
-    d_qkv = jnp.concatenate([low(d_q_pre.reshape(count, width)), low(d_k_pre), low(d_v)], axis=1)
-    dn_part = low(dot_trans(d_qkv, w_qkv))
-    d_normed = scatter_ctx(dn_part.reshape(slots, rows, -1), 7)
-    grad_qkv = low(outer_rows(normed, d_qkv))
+    moved = dict(
+        dm=dm_out,
+        back=middle_low.reshape(slots, -1, HEAD_SIZE),
+        gate=grad_gate.reshape(4, -1, 2 * ff_half),
+        up=grad_up.reshape(4, -1, 2 * ff_half),
+        down=grad_dn.reshape(2, -1, MODEL_WIDTH),
+        oproj=grad_o.reshape(4, -1, MODEL_WIDTH),
+    )
+    loaded = dict(
+        tok=tokens[0],
+        a_gain=a_gain[None],
+        dg2=jnp.sum(dg2, axis=0)[None],
+        q=q_low.reshape(count, width),
+        k=k_low,
+        kt=jnp.transpose(k_low),
+        v=v_low,
+        mixed=jnp.transpose(mixed, (1, 0, 2)).reshape(count, width),
+        lse=log_total.reshape(2, 1, count),
+        first=first[None],
+        dealt=dealt_index[None],
+        q_pre=qkv[:, :width],
+        k_pre=k_pre,
+        q_gain=q_gain[None],
+        k_gain=k_gain_all[None],
+        cos=cosine,
+        sin=sine * jnp.where(jnp.arange(HEAD_SIZE) < HEAD_SIZE // 2, -1.0, 1.0),
+        normed=normed,
+        w_qkv=w_qkv,
+    )
+    sums = back_kernel((rows, count, piece), 6)(moved, loaded)
 
     own_plan = lax.dynamic_index_in_dim(plan, here, 0, keepdims=False)
-    d_middle_given = jnp.take(back[:, :piece], own_plan, axis=0).reshape(rows, MODEL_WIDTH)
-    dx1, dg1 = norm_back(tokens[0].astype(jnp.float32), a_gain, d_normed)
-    input_grad = d_middle_given.astype(jnp.float32) + dx1
-
-    gain_sums = lax.psum(
-        jnp.concatenate(
-            [
-                jnp.sum(dg1, axis=0).reshape(4, 256),
-                jnp.sum(dg2, axis=0).reshape(4, 256),
-                jnp.sum(dg_q, axis=(0, 1)).reshape(4, 32),
-                jnp.sum(dg_k, axis=0).reshape(4, 32),
-            ],
-            axis=1,
-        ),
-        ("z", "y", "x", "core"),
-    )
-    own_gain = lax.dynamic_index_in_dim(gain_sums, 2 * x + core, 0, keepdims=False)
-
-    def halves(a):
-        return a.reshape(2, a.shape[0] // 2, *a.shape[1:])
-
-    def by_core(a):
-        return jnp.swapaxes(a.reshape(2, 2, -1, a.shape[-1]), 0, 1)
-
-    gu_half = half_sum(halves(grad_gu), "x")
-    gu_blocks = jnp.swapaxes(gu_half.reshape(2, LINE, -1, 4 * ff_half), 0, 1)
-    dn_half = half_sum(halves(grad_dn), "x").reshape(LINE, -1, MODEL_WIDTH)
-    o_half = half_sum(half_sum(by_core(grad_o), "core"), "x").reshape(slots, -1, MODEL_WIDTH)
-    qkv_sum = half_sum(half_sum(by_core(grad_qkv), "core"), "x")
-    gu_all, dn_all, o_all, qkv_all = sum_and_gather(gu_blocks, dn_half, o_half, qkv_sum, 8)
-    q_all = jnp.transpose(qkv_all[:, :, :width], (1, 0, 2)).reshape(-1, slots * width)
-    k_all = jnp.transpose(qkv_all[:, :, width : width + HEAD_SIZE], (1, 0, 2))
-    v_all = jnp.transpose(qkv_all[:, :, width + HEAD_SIZE :], (1, 0, 2))
-    o_sum = o_all.reshape(-1, MODEL_WIDTH)
-    gu_all = gu_all.reshape(LINE, 2, 2, -1, 2, 2, ff_half)
-    gu_all = jnp.transpose(gu_all, (4, 0, 3, 5, 2, 1, 6)).reshape(2, -1, 8 * ff_half)
-    dn_all = jnp.swapaxes(dn_all.reshape(LINE, 2, -1, MODEL_WIDTH), 0, 1).reshape(-1, MODEL_WIDTH)
-
-    def wide(a):
-        return a.astype(jnp.float32)
-
+    back = sums.back.reshape(slots, piece, MODEL_WIDTH)
+    d_middle_given = jnp.take(back, own_plan, axis=0).reshape(rows, MODEL_WIDTH)
+    input_grad = d_middle_given.astype(jnp.float32) + sums.dx1
+
+    place = 2 * x + core
+
+    def own_part(start, size):
+        part = sums.gains[0, start : start + size]
+        return lax.dynamic_slice_in_dim(part, place * (size // 4), size // 4)
+
+    gate_sum, up_sum, down_sum, o_sum, q_sum, k_sum, v_sum = widen(
+        sums.gate, sums.up, sums.down, sums.o, sums.heads
+    )
     return (
         output[None],
         input_grad[None],
-        own_gain[:256],
-        own_gain[512:544],
-        own_gain[544:576],
-        own_gain[256:512],
-        wide(q_all),
-        wide(k_all.reshape(-1, slots * HEAD_SIZE)),
-        wide(v_all.reshape(-1, slots * HEAD_SIZE)),
-        wide(o_sum),
-        wide(gu_all[0]),
-        wide(gu_all[1]),
-        wide(dn_all),
+        own_part(0, MODEL_WIDTH),
+        own_part(2 * MODEL_WIDTH, HEAD_SIZE),
+        own_part(2 * MODEL_WIDTH + HEAD_SIZE, HEAD_SIZE),
+        own_part(MODEL_WIDTH, MODEL_WIDTH),
+        q_sum,
+        k_sum,
+        v_sum,
+        o_sum,
+        gate_sum,
+        up_sum,
+        down_sum,
     )
 
 

time: 596 us -> 446 us (0.75)
  blocking collectives: 50.2 us -> 5.82 us
  local copies, waits for them, and re-layouts: 60.8 us -> 27.7 us
  matrix products: 72.7 us -> 45.2 us
  waiting for transfers between devices: 19.2 us -> 0.74 us
  Pallas kernels: 316 us -> 302 us
    psum x1 -> x0, blocking collectives: 44.3 us -> none  [fast_layer(): lax.psum(jnp.concatenate([jnp.sum(dg1, axis=0).reshape(4, 256), jnp.sum(d...]
    pallas_call x9 -> x7, Pallas kernels: 316 us -> 293 us  [net_call(): pl.pallas_call(kernel, out_shape=outs, in_specs=[in_vmem if i in vmem els...]
    dot_general x5 -> x0, matrix products: 19.7 us -> none  [the longest x1 7.12 us: fast_layer(): jnp.einsum('tgh,uh->gtu', d_heads, v_low, preferred_element_type=jnp.floa...]
    convert_element_type x8 -> x0, local copies, waits for them, and re-layouts: 18.5 us -> none  [wide(): return a.astype(jnp.float32)]
    ppermute x6 -> x0, waiting for transfers between devices: 18.5 us -> none  [over(): return lax.ppermute(block, axis, [(0, 1), (1, 0)])]
    unnamed x121 -> x75, local copies, waits for them, and re-layouts: 14 us -> 1.88 us
    convert_element_type x5 -> x0, other arithmetic: 11.2 us -> none  [wide(): return a.astype(jnp.float32)]
    pallas_call x0 -> x1, Pallas kernels: none -> 8.98 us  [widen(): pl.pallas_call(kernel, grid=(LINE,), in_specs=[pl.BlockSpec((2, 2, z_gu,...]
  transfers between devices with their start and end apart: 9 -> 3, of which waited for: 2 -> 0; matrix products, arithmetic and copies ran while one was open for 12% -> 18% of each run, Pallas kernels for 20% -> 18%
where the time goes in v3:
time: 446 us; the launch traced here: 440 us
  Pallas kernels  302 us (68%)
  matrix products  45.2 us (10%)
  other arithmetic  43.3 us (10%)
  local copies, waits for them, and re-layouts  27.7 us (6%)
  between operations  14.9 us (3%)
  blocking collectives  5.82 us (1%)
    pallas_call x7, Pallas kernels, net_call(): pl.pallas_call(kernel, out_shape=outs, in_specs=[in_vmem if i in vmem els...  293 us
    dot_general x6, matrix products, dot(): return jnp.dot(a, b, preferred_element_type=jnp.float32)  17.2 us
    convert_element_type x6, other arithmetic, low(): return a.astype(jnp.bfloat16)  16.3 us
    dot_general x4, matrix products, outer_rows(): lax.dot_general(left_side, right_side, (((0,), (0,)), ((), ())), preferre...  12.4 us
    dot_general x3, matrix products, dot_trans(): lax.dot_general(left_side, right_side, (((1,), (1,)), ((), ())), preferre...  9.36 us
    pallas_call x1, Pallas kernels, widen(): pl.pallas_call(kernel, grid=(LINE,), in_specs=[pl.BlockSpec((2, 2, z_gu,...  8.98 us
  transfers between devices with their start and end apart: 3, of which 0 were waited for; matrix products, arithmetic and copies ran while one was open for 18% of the time, Pallas kernels for 18%

profile of v3, /device:TPU:0, one launch (start us, length us, event | category | flops | bytes accessed | tf_op | source)
XLA Modules:
  0.0 439.9 jit_solution(12410479260152762854)
XLA Ops:
  9.9 5.8 %all_to_all.5 = bf16[2,256,1536]{2,1,0:T(8,128)(2,1)} all-to-all(bf16[2,256,1536]{2,1,0:T(8,128)(2,1)S(1)} %pad_maximum_fusion), channel_id=1, replica_groups=mesh['z'=4,'y'=2,'x'=2,'core'=2] {'core'}, dimensions={0} | all-to-all | bytes 3145728 | tf_op jit(solution)/shard_map/all_to_all | solution.py:1522
  20.1 39.8 %shard_map.246 = (bf16[8,160,1024]{2,1,0:T(8,128)(2,1)}, bf16[4,256,512]{2,1,0:T(8,128)(2,1)}, bf16[4,16,576]{2,1,0:T(8,128)(2,1)}) custom-call(bf16[160,1024]{1,0:T(8,128)(2,1)} %bitcast.158, bf16[256,512]{1,0:T(8,128)(2,1)} %pad_maximum_fusion.3.refs_1_, bf16[16,576]{1,0:T(8,128)(2,1)} %tile.2.refs_2_), custom_call_target="tpu_custom_call" | custom-call | tf_op jit(solution)/shard_map/pallas_call | solution.py:747
  61.0 2.7 fusion.6
  78.9 3.0 multiply_multiply_fusion
  88.0 8.4 %add_convert_fusion = (bf16[1280,2,128]{2,1,0:T(2,128)(2,1)S(1)}, f32[1280,2,128]{2,1,0:T(2,128)}) fusion(f32[1280,128]{1,0:T(8,128)S(1)} %get-tuple-element.70.refs_7_, f32[1280,128]{1,0:T(8,128)S(1)} %get-tuple-element.71, f32[1280,2,64]{2,1,0:T(2,128)S(1)} %get-tuple-element.67, f32[1280,2,64]{2,1,0:T(2,128)S(1)} %get-tuple-element.66, f32[128]{0:T(128)S(1)} %mul.338, ...), kind=kLoop, calls=%fused_computation.48 | loop fusion | flops 2293760 | bytes 5908992 | tf_op jit(solution)/shard_map/convert_element_type | solution.py:534
  96.5 2.8 fusion.45
  101.7 3.4 fusion.12
  110.0 14.7 %shard_map.247 = bf16[8,160,256]{2,1,0:T(8,128)(2,1)} custom-call(bf16[8,160,256]{2,1,0:T(8,128)(2,1)} %bitcast.162), custom_call_target="tpu_custom_call" | custom-call | tf_op jit(solution)/shard_map/pallas_call | solution.py:747
  126.6 13.5 %shard_map.250 = bf16[4,160,1024]{2,1,0:T(8,128)(2,1)} custom-call(bf16[160,1024]{1,0:T(8,128)(2,1)} %bitcast.155), custom_call_target="tpu_custom_call" | custom-call | tf_op jit(solution)/shard_map/pallas_call | solution.py:747
  141.1 4.0 multiply_convert_fusion.refs_17_
  146.4 3.1 mul.336
  150.9 3.2 fusion.48
  156.7 11.3 %shard_map.248 = bf16[4,160,1024]{2,1,0:T(8,128)(2,1)} custom-call(bf16[160,1024]{1,0:T(8,128)(2,1)} %multiply_convert_fusion.2.refs_0_), custom_call_target="tpu_custom_call" | custom-call | tf_op jit(solution)/shard_map/pallas_call | solution.py:747
  168.0 6.5 %fusion.49 = f32[640,1536]{1,0:T(8,128)} fusion(bf16[640,1024]{1,0:T(8,128)(2,1)} %bitcast.151, bf16[1024,1536]{1,0:T(8,128)(2,1)} %bitcast.176), kind=kOutput, calls=%fused_computation.140 | convolution fusion | flops 2013265920 | bytes 8388608 | tf_op jit(solution)/shard_map/dot_general | solution.py:530
  174.5 4.5 %fusion.20 = (bf16[640,768]{1,0:T(8,128)(2,1)S(1)}, bf16[640,768]{1,0:T(8,128)(2,1)S(1)}, bf16[640,768]{1,0:T(8,128)(2,1)S(1)}) fusion(f32[640,1536]{1,0:T(8,128)} %fusion.49, bf16[768,1024]{1,0:T(8,128)(2,1)} %all-gather.8.cloned.1.call-done, bf16[640,1024]{1,0:T(8,128)(2,1)S(1)} %bitcast.149), kind=kOutput, calls=%fused_computation.30 | convolution fusion | flops 1014005760 | bytes 9764864 | tf_op jit(solution)/shard_map/dot_general | solution.py:39
  179.1 2.6 convolution_convert_fusion.3
  181.7 3.3 fusion.23
  185.0 2.6 convolution_convert_fusion.4
  189.8 13.9 %shard_map.249 = f32[160,1024]{1,0:T(8,128)} custom-call(bf16[4,160,1024]{2,1,0:T(8,128)(2,1)} %bitcast.157), custom_call_target="tpu_custom_call" | custom-call | tf_op jit(solution)/shard_map/pallas_call | solution.py:747
  203.7 13.4 %shard_map.251 = f32[160,1024]{1,0:T(8,128)} custom-call(bf16[4,160,1024]{2,1,0:T(8,128)(2,1)} %bitcast.156), custom_call_target="tpu_custom_call" | custom-call | tf_op jit(solution)/shard_map/pallas_call | solution.py:747
  220.2 3.3 convolution_convert_fusion
  224.6 3.9 convolution_convert_fusion.5
  230.9 186.5 %shard_map.252 = (bf16[8,160,128]{2,1,0:T(8,128)(2,1)}, bf16[8,96,1024]{2,1,0:T(8,128)(2,1)}, f32[160,1024]{1,0:T(8,128)}, f32[1,2304]{1,0:T(1,128)}, bf16[8,2,6...) custom-call(bf16[8,160,128]{2,1,0:T(8,128)(2,1)} %reshape.314.refs_0, ...), custom_call_target="tpu_custom_call" | custom-call | tf_op jit(solution)/shard_map/pallas_call | solution.py:747
  423.9 9.0 %shard_map.253 = (f32[256,3072]{1,0:T(8,128)}, f32[256,3072]{1,0:T(8,128)}, f32[2,384,1024]{2,1,0:T(8,128)}, f32[512,1024]{1,0:T(8,128)}, f32[256,2048]{1,0:T(8,...) custom-call(bf16[8,2,64,768]{3,2,1,0:T(8,128)(2,1)} %get-tuple-element.37.gate, ...), custom_call_target="tpu_custom_call" | custom-call | tf_op jit(solution)/shard_map/pallas_call | solution.py:1377
  (167 shorter events, 59.8 us)
Async XLA Ops:
  7.2 8.7 %copy-start = (bf16[768,1024]{1,0:T(8,128)(2,1)S(1)}, bf16[768,1024]{1,0:T(8,128)(2,1)}, u32[]{:S(2)}) copy-start(bf16[768,1024]{1,0:T(8,128)(2,1)} %param.28) | copy-start | bytes 4718596
  7.2 143.7 %all-gather.4.cloned.1.call-start = ((), (), s32[]{:S(2)}) async-start(), calls=%async_computation.1 | async-start | bytes 5242880 | tf_op jit(solution)/shard_map/all_gather | solution.py:538
  7.9 160.1 %all-gather.6.cloned.1.call-start = ((), (), s32[]{:S(2)}) async-start(), calls=%async_computation.2 | async-start | bytes 4718592 | tf_op jit(solution)/shard_map/all_gather | solution.py:1523
  15.8 158.7 %all-gather.8.cloned.1.call-start = ((), (), s32[]{:S(2)}) async-start(), calls=%async_computation.3 | async-start | bytes 2359296 | tf_op jit(solution)/shard_map/all_gather | solution.py:1525
  15.8 3.6 copy-start.27
  59.9 3.8 copy-start.2
  66.7 8.9 %copy-start.5 = (f32[1280,256]{1,0:T(8,128)}, f32[1280,256]{1,0:T(8,128)S(1)}, u32[]{:S(2)}) copy-start(f32[1280,256]{1,0:T(8,128)S(1)} %slice.81.refs_20_) | copy-start | bytes 3932164
  66.7 7.8 %copy-start.26 = (s32[1,8,8]{2,1,0:T(8,128)S(1)}, s32[1,8,8]{2,1,0:T(8,128)}, u32[]{:S(2)}) copy-start(s32[1,8,8]{2,1,0:T(8,128)} %param.17) | copy-start | bytes 772
  78.9 9.1 %copy-start.8 = (f32[1280,2]{1,0:T(8,128)}, f32[1280,2]{1,0:T(8,128)S(1)}, u32[]{:S(2)}) copy-start(f32[1280,2]{1,0:T(8,128)S(1)} %add_rsqrt_fusion) | copy-start | bytes 30724
  88.0 8.4 %copy-start.6 = (f32[1280,128]{1,0:T(8,128)}, f32[1280,128]{1,0:T(8,128)S(1)}, u32[]{:S(2)}) copy-start(f32[1280,128]{1,0:T(8,128)S(1)} %get-tuple-element.70.refs_7_) | copy-start | bytes 1966084
  88.0 52.1 %copy-start.17 = (bf16[1280,128]{1,0:T(8,128)(2,1)}, bf16[1280,128]{1,0:T(8,128)(2,1)S(1)}, u32[]{:S(2)}) copy-start(bf16[1280,128]{1,0:T(8,128)(2,1)S(1)} %get-tuple-element.69.refs_11_) | copy-start | bytes 983044
  88.0 8.4 %copy-start.19 = (pred[1280,1280]{0,1:T(8,128)(4,1)S(1)}, pred[1280,1280]{0,1:T(8,128)(4,1)}, u32[]{:S(2)}) copy-start(pred[1280,1280]{0,1:T(8,128)(4,1)} %fusion.5) | copy-start | bytes 4915204
  105.5 4.5 %copy-start.15 = (f32[1280,256]{1,0:T(8,128)}, f32[1280,256]{1,0:T(8,128)S(1)}, u32[]{:S(2)}) copy-start(f32[1280,256]{1,0:T(8,128)S(1)} %copy.89.refs_16_) | copy-start | bytes 3932164
  141.1 4.8 %copy-start.7 = (f32[1280,128]{1,0:T(8,128)S(1)}, f32[1280,128]{1,0:T(8,128)}, u32[]{:S(2)}) copy-start(f32[1280,128]{1,0:T(8,128)} %copy-done.6) | copy-start | bytes 1966084
  141.1 8.4 %copy-start.16 = (f32[1280,2,128]{2,1,0:T(2,128)S(1)}, f32[1280,2,128]{2,1,0:T(2,128)}, u32[]{:S(2)}) copy-start(f32[1280,2,128]{2,1,0:T(2,128)} %get-tuple-element.52) | copy-start | bytes 3932164
  145.9 3.6 copy-start.13
  168.0 6.5 %copy-start.20 = (bf16[4,160,1024]{2,1,0:T(8,128)(2,1)S(1)}, bf16[4,160,1024]{2,1,0:T(8,128)(2,1)}, u32[]{:S(2)}) copy-start(bf16[4,160,1024]{2,1,0:T(8,128)(2,1)} %shard_map.250) | copy-start | bytes 3932164
  174.5 4.6 %copy-start.22 = (bf16[4,160,1024]{2,1,0:T(8,128)(2,1)S(1)}, bf16[4,160,1024]{2,1,0:T(8,128)(2,1)}, u32[]{:S(2)}) copy-start(bf16[4,160,1024]{2,1,0:T(8,128)(2,1)} %shard_map.248) | copy-start | bytes 3932164
  179.1 8.5 %copy-start.34 = (bf16[640,768]{1,0:T(8,128)(2,1)}, bf16[640,768]{1,0:T(8,128)(2,1)S(1)}, u32[]{:S(2)}) copy-start(bf16[640,768]{1,0:T(8,128)(2,1)S(1)} %get-tuple-element.55) | copy-start | bytes 2949124
  203.7 15.4 %copy-start.23 = (bf16[1,160,1024]{2,1,0:T(8,128)(2,1)S(1)}, bf16[1,160,1024]{2,1,0:T(8,128)(2,1)}, u32[]{:S(2)}) copy-start(bf16[1,160,1024]{2,1,0:T(8,128)(2,1)} %param.29) | copy-start | bytes 983044
  220.2 4.4 copy-start.21
  224.6 3.9 copy-start.4
  417.4 5.6 %copy-start.25 = (f32[160,1024]{1,0:T(8,128)S(1)}, f32[160,1024]{1,0:T(8,128)}, u32[]{:S(2)}) copy-start(f32[160,1024]{1,0:T(8,128)} %get-tuple-element.35) | copy-start | bytes 1966084
  423.9 9.0 %copy-start.1 = (bf16[768,1024]{1,0:T(8,128)(2,1)S(1)}, bf16[768,1024]{1,0:T(8,128)(2,1)}, u32[]{:S(2)}) copy-start(bf16[768,1024]{1,0:T(8,128)(2,1)} %param.28) | copy-start | bytes 4718596
  (14 other events, 32.2 us)
Sparse Core Ops, SparseCore 0:
  9.6 40.1 all-gather.3
  51.4 46.9 all-gather.5
  100.4 27.2 all-gather.7
